TPU v7x, 256 devices: a whole 4x4x8 slice. The times are simulated.
256 devices in a mesh: ens: 8 (over z), space: 32 (over x, y, core).
Axes of the slice: x: 4, y: 4, z: 8, core: 2. Of those that a mesh axis runs over, the one named last changes fastest.
Arguments:
- initial_states: bfloat16 [8, 100, 98304], P('ens', None, 'space'), may hold values from -6 to 6
- owner: int32 [98304, 1], P('space'), may hold values from 0 to 31; in each aligned block of 3072 rows (0 to 3071, 3072 to 6143, ...) at most 192 rows name the same one
- node_local: int32 [98304], P('space'), may hold values from 0 to 127
- adjacent_vertex_ids: int32 [4096, 16], P('space'), may hold values from 0 to 4095, as said below
- vertex_latents: bfloat16 [4096, 1024], P('space'), may hold values from -6 to 6
- norm_factor: float32 [1024], replicated, may hold values from 0.1 to 1.9
- grid_to_mesh_matrix: bfloat16 [100, 1024], replicated, may hold values from -0.625 to 0.625
- receiver_matrix: bfloat16 [1024, 1024], replicated, may hold values from -0.1875 to 0.1875
- sender_matrix: bfloat16 [1024, 1024], replicated, may hold values from -0.1875 to 0.1875
- link_update_matrix: bfloat16 [1024, 1024], replicated, may hold values from -0.1875 to 0.1875
- mesh_to_grid_matrix: bfloat16 [1024, 100], replicated, may hold values from -0.1875 to 0.1875
- observed: float32 [100, 98304], P(None, 'space'), may hold values from -6 to 6
- area: float32 [98304], P('space'), may hold values from 0.5 to 2
Outputs:
- crps: float32 [100, 98304], P(None, ('space', 'ens'))
- grads: float32 [8, 100, 98304], P('ens', None, 'space')
Inputs may be any that keep to these rules, and one draw needn't show every extreme that they name: Among the grid points of one index of space, at most 192 name one owner, and in every draw some owner is named exactly 192 times by one index's points. `adjacent_vertex_ids`: each neighbour of a node lies on the node's own index of space or on the one just before or after it, cyclically: its id divided by 128 is within one of the node's id divided by 128, modulo 32.
All inputs are finite; a program needn't handle non-finite values.
Results may differ from a plain program's by a relative error of at most 0.02.
Values may be sent and summed in bfloat16 or wider, within the bound.
No kernel may reach another device: no remote copies, remote signals or barrier semaphores. Data moves between devices by JAX's collectives and lax.ppermute only.
A program may use at most 128 MiB of HBM per device.

v0:
```python
import functools

import jax
import jax.numpy as jnp
from jax import lax
from jax.experimental import pallas as pl
from jax.experimental.pallas import tpu as pltpu
from jax.sharding import PartitionSpec as P

SLOTS = 192
LANE = 128
PART = 13
PAD = 16
BF16, F32 = jnp.bfloat16, jnp.float32
VM = pl.BlockSpec(memory_space=pltpu.VMEM)
SM = pl.BlockSpec(memory_space=pltpu.SMEM)


ANY = pl.BlockSpec(memory_space=pl.ANY)


def cost(flops, moved, transcendentals=0):
    return pl.CostEstimate(flops=int(flops), bytes_accessed=int(moved), transcendentals=int(transcendentals))


def params(mib):
    return pltpu.CompilerParams(vmem_limit_bytes=mib * 2**20)


def pack_kernel(core_ref, own_ref, owner_ref, local_ref, slots_ref, ids_ref, wide, rows, slots, pos_v, pos_s, sem):
    variables = own_ref.shape[0]
    blocks = owner_ref.shape[0]
    spaces = slots.shape[0] // SLOTS
    row = lax.broadcasted_iota(jnp.int32, (LANE, 2 * LANE), 0)
    col = lax.broadcasted_iota(jnp.int32, (LANE, 2 * LANE), 1)
    before = jnp.where((row < col) | (col >= LANE), 1.0, 0.0).astype(BF16)
    names = lax.broadcasted_iota(jnp.int32, (spaces, LANE), 0)
    carry = jnp.zeros((spaces, LANE), F32)
    for j in range(blocks):
        owner = owner_ref[j : j + 1, :]
        hot = jnp.where(names == owner, 1.0, 0.0)
        counts = jnp.dot(hot.astype(BF16), before, preferred_element_type=F32)
        rank = jnp.sum(hot * (counts[:, :LANE] + carry), axis=0, keepdims=True)
        carry = carry + counts[:, LANE:]
        pos_v[j : j + 1, :] = owner * SLOTS + rank.astype(jnp.int32)
    side = jnp.where(owner_ref[...] % 2 == core_ref[0], 0, spaces // 2)
    ids_ref[...] = (side + owner_ref[...] // 2) * LANE + local_ref[...]
    copy = pltpu.make_async_copy(pos_v, pos_s, sem)
    copy.start()
    slots[...] = jnp.zeros_like(slots)
    wide[variables:, :] = jnp.zeros((LANE - variables, wide.shape[1]), F32)
    wide[:variables, :] = own_ref[...].astype(F32)
    for j in range(blocks):
        wide[variables : variables + 1, j * LANE : (j + 1) * LANE] = local_ref[j : j + 1, :].astype(F32)
    for j in range(blocks):
        rows[j * LANE : (j + 1) * LANE, :] = wide[:, j * LANE : (j + 1) * LANE].T
    copy.wait()

    def place(j, _):
        for i in range(0, LANE, 16):
            base = pl.multiple_of(j * LANE + i, 16)
            held = [rows[pl.ds(base + k, 1), :] for k in range(16)]
            for k in range(16):
                slots[pl.ds(pos_s[j, i + k], 1), :] = held[k]
        return 0

    lax.fori_loop(0, blocks, place, 0)
    slots_ref[...] = slots[...].astype(BF16)


def spread_kernel(own_ref, after_ref, parts_ref, wide):
    variables = own_ref.shape[0]
    wide[...] = own_ref[...].astype(F32)
    for c in range(parts_ref.shape[0]):
        held = min(PART, variables - c * PART)
        piece = wide[c * PART : c * PART + held, :]
        parts_ref[c] = jnp.concatenate([piece, jnp.zeros((PAD - held, wide.shape[1]), F32)], axis=0).astype(BF16)


def encode_kernel(
    slots_ref,
    embed_ref,
    latent_ref,
    gain_ref,
    receiver_ref,
    sender_ref,
    normed_ref,
    query_ref,
    source_ref,
    turned,
    total,
    receiver,
    sender,
    sems,
):
    copies = [
        pltpu.make_async_copy(sender_ref, sender, sems.at[0]),
        pltpu.make_async_copy(receiver_ref, receiver, sems.at[1]),
    ]
    for copy in copies:
        copy.start()
    variables = embed_ref.shape[0]
    width = embed_ref.shape[1]
    chunk = 512
    half = jnp.concatenate([embed_ref[...].astype(F32) * 0.5, jnp.zeros((LANE - variables, width), F32)], axis=0)
    turned[...] = half.T.astype(BF16)
    total[...] = jnp.zeros_like(total)
    lanes = lax.broadcasted_iota(jnp.int32, (chunk, LANE), 1).astype(F32)

    def step(c, _):
        x = slots_ref[pl.ds(pl.multiple_of(c * chunk, chunk), chunk), :]
        h = lax.dot_general(turned[...], x, (((1,), (1,)), ((), ())), preferred_element_type=F32)
        act = (h + h * jnp.tanh(h)).astype(BF16)
        node = x[:, variables : variables + 1].astype(F32)
        hot = jnp.where(node == lanes, 1.0, 0.0).astype(BF16)
        total[...] += jnp.dot(act, hot, preferred_element_type=F32)
        return 0

    lax.fori_loop(0, slots_ref.shape[0] // chunk, step, 0)
    state = latent_ref[...].astype(F32) + total[...].T
    centred = state - jnp.mean(state, axis=-1, keepdims=True)
    spread = jnp.mean(centred * centred, axis=-1, keepdims=True)
    normed = (centred * lax.rsqrt(spread + 1e-05) * gain_ref[...]).astype(BF16)
    normed_ref[...] = normed
    copies[0].wait()
    source_ref[...] = jnp.dot(normed, sender[...], preferred_element_type=F32).astype(BF16)
    copies[1].wait()
    query_ref[...] = jnp.dot(normed, receiver[...], preferred_element_type=F32)


def process_kernel(
    near_ref,
    query_ref,
    normed_ref,
    sibling_ref,
    own_ref,
    other_ref,
    link_ref,
    decode_ref,
    behind_ref,
    out_ref,
    beside,
    total,
    spaced,
    link,
    sem,
):
    copy = pltpu.make_async_copy(link_ref, link, sem)
    copy.start()
    nodes, fanout = near_ref.shape
    variables = decode_ref.shape[1]
    group = 4
    beside[:nodes, :] = sibling_ref[...]
    beside[nodes : 2 * nodes, :] = own_ref[...]
    beside[2 * nodes :, :] = other_ref[...]
    lanes = lax.broadcasted_iota(jnp.int32, (nodes, 3 * nodes), 1)
    for g in range(0, fanout, group):
        hot = jnp.concatenate(
            [jnp.where(near_ref[:, k : k + 1] == lanes, 1.0, 0.0) for k in range(g, g + group)], axis=0
        ).astype(BF16)
        picked = jnp.dot(hot, beside[...], preferred_element_type=F32)
        h = 0.5 * (picked + jnp.concatenate([query_ref[...]] * group, axis=0))
        edge = (h + h * jnp.tanh(h)).astype(BF16)
        if g == 0:
            copy.wait()
        z = jnp.dot(edge, link[...], preferred_element_type=F32)
        z = z + z * jnp.tanh(0.5 * z)
        part = sum(z[k * nodes : (k + 1) * nodes] for k in range(group))
        if g == 0:
            total[...] = part
        else:
            total[...] += part
    updated = (normed_ref[...].astype(F32) + total[...] * (0.5 / fanout)).astype(BF16)
    decoded = lax.dot_general(decode_ref[...], updated, (((0,), (1,)), ((), ())), preferred_element_type=F32)
    spaced[...] = jnp.zeros_like(spaced)
    for c in range(out_ref.shape[0]):
        held = min(PART, variables - c * PART)
        spaced[c * PAD : c * PAD + held, :] = decoded[c * PART : c * PART + held, :]
    for c in range(out_ref.shape[0]):
        out_ref[c] = spaced[c * PAD : (c + 1) * PAD, :].astype(BF16)


def crps_kernel(
    member_ref,
    ids_ref,
    table_ref,
    other_ref,
    parts_ref,
    observed_ref,
    area_ref,
    out_ref,
    table,
    states,
    slopes,
    picked,
    held,
    seen,
):
    members = parts_ref.shape[0]
    blocks = ids_ref.shape[0]
    per_member = blocks // members
    variables = observed_ref.shape[0]
    for c in range(members):

        @pl.when(member_ref[0] == c)
        def _():
            count = min(PART, variables - c * PART)
            seen[...] = jnp.zeros_like(seen)
            seen[:count, :] = observed_ref[c * PART : c * PART + count, :]

    rows = out_ref.shape[1]
    half = table_ref.shape[0]
    table[:half, :] = table_ref[...].astype(F32)
    table[half:, :] = other_ref[...].astype(F32)
    for m in range(members):
        states[m * PAD : (m + 1) * PAD, :] = parts_ref[m].astype(F32)
        slopes[m * rows + rows - 8 : (m + 1) * rows, :] = jnp.zeros((8, LANE), F32)

    def block(j, _):
        for i in range(0, LANE, 16):
            row = [table[pl.ds(ids_ref[j, i + k], 1), :] for k in range(16)]
            for k in range(16):
                picked[i + k : i + k + 1, :] = row[k]
        here = pl.ds(pl.multiple_of(j * LANE, LANE), LANE)
        held[...] = picked[...].T + states[:, here]
        area = jnp.broadcast_to(area_ref[pl.ds(j, 1), :], (members, LANE))
        obs = seen[:, here]
        spare = j // per_member * rows + PART * blocks + j % per_member
        for v in range(PART):
            f = held[pl.ds(v, members, stride=PAD), :]
            miss = f - obs[v : v + 1, :]
            q = miss * miss + 0.01
            r = lax.rsqrt(q)
            near = q * r
            slope = None
            pairs = None
            for k in range(1, members // 2 + 1):
                d = f - pltpu.roll(f, k, 0)
                pq = d * d + 0.01
                pr = lax.rsqrt(pq)
                t = d * pr
                s = pq * pr
                if 2 * k < members:
                    t = t - pltpu.roll(t, members - k, 0)
                    s = s + s
                slope = t if slope is None else slope + t
                pairs = s if pairs is None else pairs + s
            slopes[pl.ds(v * blocks + j, members, stride=rows), :] = area * (miss * r - slope * (1.0 / (members - 1)))
            pairs = (pairs + 0.1) * (1.0 / (2.0 * members * (members - 1)))
            value = area * (near * (1.0 / members) - pairs)
            slopes[pl.ds(spare + v * per_member, 1), :] = jnp.sum(value, axis=0, keepdims=True)
        return 0

    lax.fori_loop(0, blocks, block, 0)
    for m in range(members):
        out_ref[m] = slopes[m * rows : (m + 1) * rows, :].astype(BF16)


def unpack_kernel(got_ref, crps_ref, grads_ref, wide):
    variables, points = crps_ref.shape
    parts = got_ref.shape[0]
    per_part = points // LANE
    blocks = parts * per_part
    for c in range(parts):
        wide[...] = got_ref[c].astype(F32)
        held = min(PART, variables - c * PART)
        grads_ref[c * PART * blocks : (c * PART + held) * blocks, :] = wide[: held * blocks, :]
        for j in range(per_part):
            crps_ref[c * PART : c * PART + held, j * LANE : (j + 1) * LANE] = wide[
                pl.ds(PART * blocks + j, held, stride=per_part), :
            ]


def local(
    initial_states,
    owner,
    node_local,
    adjacent_vertex_ids,
    vertex_latents,
    norm_factor,
    grid_to_mesh_matrix,
    receiver_matrix,
    sender_matrix,
    link_update_matrix,
    mesh_to_grid_matrix,
    observed,
    area,
):
    spaces = lax.axis_size("space")
    members = lax.axis_size("ens")
    variables, points = initial_states.shape[1:]
    nodes, width = vertex_latents.shape
    blocks = points // LANE
    shape = jax.ShapeDtypeStruct
    place = lax.axis_index("space")
    core = place % 2
    slots, ids = pl.pallas_call(
        pack_kernel,
        out_shape=(shape((spaces * SLOTS, LANE), BF16), shape((blocks, LANE), jnp.int32)),
        in_specs=[SM] + [VM] * 3,
        out_specs=(VM,) * 2,
        scratch_shapes=[
            pltpu.VMEM((LANE, points), F32),
            pltpu.VMEM((points, LANE), F32),
            pltpu.VMEM((spaces * SLOTS, LANE), F32),
            pltpu.VMEM((blocks, LANE), jnp.int32),
            pltpu.SMEM((blocks, LANE), jnp.int32),
            pltpu.SemaphoreType.DMA,
        ],
        compiler_params=params(24),
        cost_estimate=cost(1.5e8, 8e6),
        name="pack",
    )(core.astype(jnp.int32).reshape(1), initial_states[0], owner.reshape(blocks, LANE), node_local.reshape(blocks, LANE))
    got = lax.all_to_all(slots.reshape(spaces, SLOTS, LANE), "space", split_axis=0, concat_axis=0, tiled=True)
    parts = pl.pallas_call(
        spread_kernel,
        out_shape=shape((members, PAD, points), BF16),
        in_specs=[VM, ANY],
        out_specs=VM,
        scratch_shapes=[pltpu.VMEM((variables, points), F32)],
        compiler_params=params(8),
        cost_estimate=cost(1e6, 2e6),
        name="spread",
    )(initial_states[0], got)
    parts = lax.all_to_all(parts, "ens", split_axis=0, concat_axis=0, tiled=True)
    normed, query, source = pl.pallas_call(
        encode_kernel,
        out_shape=(shape((nodes, width), BF16), shape((nodes, width), F32), shape((nodes, width), BF16)),
        in_specs=[VM] * 4 + [ANY] * 2,
        out_specs=(VM,) * 3,
        scratch_shapes=[
            pltpu.VMEM((width, LANE), BF16),
            pltpu.VMEM((width, nodes), F32),
            pltpu.VMEM((width, width), BF16),
            pltpu.VMEM((width, width), BF16),
            pltpu.SemaphoreType.DMA((2,)),
        ],
        compiler_params=params(32),
        cost_estimate=cost(4e9, 8e6, 6.3e6),
        name="encode",
    )(
        got.reshape(spaces * SLOTS, LANE),
        grid_to_mesh_matrix,
        vertex_latents,
        norm_factor.reshape(1, width),
        receiver_matrix,
        sender_matrix,
    )
    sibling = lax.ppermute(source, "space", [(i, i ^ 1) for i in range(spaces)])
    other = lax.ppermute(source, "space", [(i, (i + 2 * (i % 2) - 1) % spaces) for i in range(spaces)])
    home = adjacent_vertex_ids // nodes
    slab = jnp.where(home == place, 1, jnp.where(home == place + 1 - 2 * core, 0, 2))
    near = slab * nodes + adjacent_vertex_ids % nodes
    decoded = pl.pallas_call(
        process_kernel,
        out_shape=shape((members, PAD, nodes), BF16),
        in_specs=[VM] * 6 + [ANY, VM, ANY],
        out_specs=VM,
        scratch_shapes=[
            pltpu.VMEM((3 * nodes, width), BF16),
            pltpu.VMEM((nodes, width), F32),
            pltpu.VMEM((members * PAD, nodes), F32),
            pltpu.VMEM((width, width), BF16),
            pltpu.SemaphoreType.DMA,
        ],
        compiler_params=params(32),
        cost_estimate=cost(6e9, 4e6, 4.2e6),
        name="process",
    )(near, query, normed, sibling, source, other, link_update_matrix, mesh_to_grid_matrix, parts)
    decoded = lax.all_to_all(decoded, "ens", split_axis=0, concat_axis=0, tiled=True)
    decoded = decoded.reshape(members * PAD, nodes).T
    table = lax.all_to_all(
        jnp.broadcast_to(decoded[None], (spaces // 2, nodes, members * PAD)),
        "space",
        split_axis=0,
        concat_axis=0,
        tiled=True,
        axis_index_groups=[list(range(c, spaces, 2)) for c in range(2)],
    ).reshape(spaces // 2 * nodes, members * PAD)
    table_other = lax.ppermute(table, "space", [(i, i ^ 1) for i in range(spaces)])
    rows = -(-PART * (blocks + blocks // members) // 16) * 16
    slopes = pl.pallas_call(
        crps_kernel,
        out_shape=shape((members, rows, LANE), BF16),
        in_specs=[SM, SM] + [VM] * 5,
        out_specs=VM,
        scratch_shapes=[
            pltpu.VMEM((spaces * nodes, LANE), F32),
            pltpu.VMEM((members * PAD, points), F32),
            pltpu.VMEM((members * rows, LANE), F32),
            pltpu.VMEM((LANE, LANE), F32),
            pltpu.VMEM((members * PAD, LANE), F32),
            pltpu.VMEM((PAD, points), F32),
        ],
        compiler_params=params(24),
        cost_estimate=cost(5e9, 6e6, 2e6),
        name="crps",
    )(
        lax.axis_index("ens").astype(jnp.int32).reshape(1),
        ids,
        table,
        table_other,
        parts,
        observed,
        area.reshape(blocks, LANE),
    )
    slopes = lax.all_to_all(slopes, "ens", split_axis=0, concat_axis=0, tiled=True)
    crps, grads = pl.pallas_call(
        unpack_kernel,
        out_shape=(shape((variables, points // members), F32), shape((variables * blocks, LANE), F32)),
        in_specs=[VM],
        out_specs=(VM, VM),
        scratch_shapes=[pltpu.VMEM((rows, LANE), F32)],
        compiler_params=params(16),
        cost_estimate=cost(1e6, 2e6),
        name="unpack",
    )(slopes)
    return crps, grads.reshape(1, variables, points)


def solution(mesh):
    return jax.shard_map(
        local,
        mesh=mesh,
        in_specs=(
            P("ens", None, "space"),
            P("space", None),
            P("space"),
            P("space", None),
            P("space", None),
            P(),
            P(),
            P(),
            P(),
            P(),
            P(),
            P(None, "space"),
            P("space"),
        ),
        out_specs=(P(None, ("space", "ens")), P("ens", None, "space")),
        check_vma=False,
    )
```

profile of v0, /device:TPU:1, one launch (start us, length us, event | category | flops | bytes accessed | tf_op | source)
XLA Modules:
  0.0 148.8 jit_solution(9045079342815663868)
XLA Ops:
  0.6 0.0 copy-start
  0.7 1.1 copy-done
  1.7 0.0 copy-start.1
  1.7 0.7 copy-done.1
  2.4 0.7 copy-done.2
  3.1 4.0 %pack.1 = (bf16[6144,128]{1,0:T(8,128)(2,1)S(1)}, s32[24,128]{1,0:T(8,128)S(1)}) custom-call(s32[1]{0:T(128)} %bitcast.1.core_ref, bf16[100,3072]{1,0:T(8,128)(2,1)S(1)} %bitcast.15, s32[24,128]{1,0:T(8,128)S(1)} %bitcast.20, s32[24,128]{1,0:T(8,128)S(1)} %bitcast.21), custom_call_target="tpu_custom_call" | custom-call | flops 150000000 | bytes 8000000 | tf_op jit(solution)/shard_map/pack/pallas_call | solution.py:297
  7.2 31.2 %all_to_all.25.after_ref = bf16[32,192,128]{2,1,0:T(8,128)(2,1)S(1)} all-to-all(bf16[32,192,128]{2,1,0:T(8,128)(2,1)S(1)} %bitcast.17), channel_id=1, replica_groups=mesh['ens'=8,'space'=32] {'space'}, dimensions={0} | all-to-all | bytes 3145728 | tf_op jit(solution)/shard_map/all_to_all | solution.py:314
  38.4 0.0 copy-start.7
  38.4 0.0 copy-start.8
  38.4 0.0 copy-start.10
  38.4 1.1 spread.1
  39.5 8.2 %all-to-all-start.1 = ((bf16[8,16,3072]{2,1,0:T(8,128)(2,1)}), bf16[8,16,3072]{2,1,0:T(8,128)(2,1)S(1)}, u32[]{:S(2)}, u32[]{:S(2)}) async-start(bf16[8,16,3072]{2,1,0:T(8,128)(2,1)} %spread.1), calls=%async_computation.1 | async-start | bytes 1572864 | tf_op jit(solution)/shard_map/all_to_all | solution.py:325
  47.7 0.0 copy-done.7
  47.7 0.0 copy-done.8
  47.7 0.0 copy-done.10
  47.7 0.0 copy-start.3
  47.8 1.6 %copy-done.3 = bf16[1024,1024]{1,0:T(8,128)(2,1)S(1)} copy-done((bf16[1024,1024]{1,0:T(8,128)(2,1)S(1)}, bf16[1024,1024]{1,0:T(8,128)(2,1)}, u32[]{:S(2)}) %copy-start.3) | copy-done | bytes 2097176
  49.3 0.0 copy-start.4
  49.3 1.6 %copy-done.4 = bf16[1024,1024]{1,0:T(8,128)(2,1)S(1)} copy-done((bf16[1024,1024]{1,0:T(8,128)(2,1)S(1)}, bf16[1024,1024]{1,0:T(8,128)(2,1)}, u32[]{:S(2)}) %copy-start.4) | copy-done | bytes 2097176
  50.9 0.0 copy-start.13
  50.9 10.3 %encode.1 = (bf16[128,1024]{1,0:T(8,128)(2,1)S(1)}, f32[128,1024]{1,0:T(8,128)S(1)}, bf16[128,1024]{1,0:T(8,128)(2,1)S(1)}) custom-call(bf16[6144,128]{1,0:T(8,128)(2,1)S(1)} %bitcast.14, bf16[100,1024]{1,0:T(8,128)(2,1)S(1)} %copy-done.8, bf16[128,1024]{1,0:T(8,128)(2,1)S(1)} %copy-done.7, f32[1,1024]{1,0:T(1,128)S(1)} %bitcast.23, ...), custom_call_target="tpu_custom_call" | custom-call | flops 4000000000 | bytes 8000000 | tf_op jit(solution)/shard_map/encode/pallas_call | solution.py:326
  61.3 0.0 copy-start.11
  61.3 0.8 copy-done.11
  62.1 0.4 collective-permute-start.1
  62.5 1.6 %collective-permute-start = (bf16[128,1024]{1,0:T(8,128)(2,1)S(1)}, bf16[128,1024]{1,0:T(8,128)(2,1)S(1)}, u32[]{:S(2)}, u32[]{:S(2)}) collective-permute-start(bf16[128,1024]{1,0:T(8,128)(2,1)S(1)} %get-tuple-element.13.own_ref), channel_id=1, source_target_pairs={{0,1},{1,0},{2,3},{3,2},{4,5},{5,4},{6,7},{7,6},{8,9},{9,8},{10,11... | collective-permute-start | bytes 786440 | tf_op jit(solution)/shard_map/ppermute | solution.py:349
  64.1 0.0 copy-done.13
  64.1 0.1 copy.22
  64.2 1.1 copy.26.decode_ref
  65.3 0.1 fusion.near_ref
  65.4 2.7 %collective-permute-done.1.other_ref = bf16[128,1024]{1,0:T(8,128)(2,1)S(1)} collective-permute-done((bf16[128,1024]{1,0:T(8,128)(2,1)S(1)}, bf16[128,1024]{1,0:T(8,128)(2,1)S(1)}, u32[]{:S(2)}, u32[]{:S(2)}) %collective-permute-start.1) | collective-permute-done | bytes 262176 | tf_op jit(solution)/shard_map/ppermute | solution.py:350
  68.2 0.0 collective-permute-done.sibling_ref
  68.2 3.2 %all-to-all-done.1.behind_ref.parts_ref = bf16[8,16,3072]{2,1,0:T(8,128)(2,1)S(1)} async-done(((bf16[8,16,3072]{2,1,0:T(8,128)(2,1)}), bf16[8,16,3072]{2,1,0:T(8,128)(2,1)S(1)}, u32[]{:S(2)}, u32[]{:S(2)}) %all-to-all-start.1) | async-done | bytes 786464 | tf_op jit(solution)/shard_map/all_to_all | solution.py:325
  71.4 0.0 copy-start.5
  71.4 1.6 %copy-done.5 = bf16[1024,1024]{1,0:T(8,128)(2,1)S(1)} copy-done((bf16[1024,1024]{1,0:T(8,128)(2,1)S(1)}, bf16[1024,1024]{1,0:T(8,128)(2,1)}, u32[]{:S(2)}) %copy-start.5) | copy-done | bytes 2097176
  73.0 1.0 copy-done.12
  74.0 8.2 %process.1 = bf16[8,16,128]{2,1,0:T(8,128)(2,1)S(1)} custom-call(s32[128,16]{1,0:T(8,128)S(1)} %fusion.near_ref, f32[128,1024]{1,0:T(8,128)S(1)} %copy-done.12, bf16[128,1024]{1,0:T(8,128)(2,1)S(1)} %get-tuple-element.12.normed_ref, bf16[128,1024]{1,0:T(8,128)(2,1)S(1)} %collective-permute-done.sibling_ref, bf16[128,1024]{1,0:T(8,128)(2,1)S(1)} %get-tuple-element.13.own_ref, ...), custom_call_target="tpu_custom_call" | custom-call | flops 6000000000 | bytes 4000000 | tf_op jit(solution)/shard_map/process/pallas_call | solution.py:354
  82.2 0.0 copy-start.9
  82.3 9.8 %all_to_all.26 = bf16[8,16,128]{2,1,0:T(8,128)(2,1)S(1)} all-to-all(bf16[8,16,128]{2,1,0:T(8,128)(2,1)S(1)} %process.1), channel_id=1, replica_groups=mesh['ens'=8,'space'=32] {'ens'}, dimensions={0} | all-to-all | bytes 65536 | tf_op jit(solution)/shard_map/all_to_all | solution.py:370
  92.1 0.1 copy.27
  92.2 0.1 broadcast_in_dim.15
  92.3 15.0 %all_to_all.27 = bf16[16,128,128]{2,1,0:T(8,128)(2,1)S(1)} all-to-all(bf16[16,128,128]{2,1,0:T(8,128)(2,1)S(1)} %broadcast_in_dim.15), channel_id=1, replica_groups={{0,2,4,6,8,10,12,14,16,18,20,22,24,26,28,30},{1,3,5,7,9,11,13,15,17,19,..., dimensions={0} | all-to-all | bytes 1048576 | tf_op jit(solution)/shard_map/all_to_all | solution.py:372
  107.3 3.6 %collective-permute-start.2 = (bf16[2048,128]{1,0:T(8,128)(2,1)S(1)}, bf16[2048,128]{1,0:T(8,128)(2,1)S(1)}, u32[]{:S(2)}, u32[]{:S(2)}) collective-permute-start(bf16[2048,128]{1,0:T(8,128)(2,1)S(1)} %bitcast.18), channel_id=1, source_target_pairs={{0,1},{1,0},{2,3},{3,2},{4,5},{5,4},{6,7},{7,6},{8,9},{9,8},{10,11... | collective-permute-start | bytes 1572872 | tf_op jit(solution)/shard_map/ppermute | solution.py:380
  110.9 1.5 %collective-permute-done.2.other_ref = bf16[2048,128]{1,0:T(8,128)(2,1)S(1)} collective-permute-done((bf16[2048,128]{1,0:T(8,128)(2,1)S(1)}, bf16[2048,128]{1,0:T(8,128)(2,1)S(1)}, u32[]{:S(2)}, u32[]{:S(2)}) %collective-permute-start.2) | collective-permute-done | bytes 524320 | tf_op jit(solution)/shard_map/ppermute | solution.py:380
  112.5 0.0 copy-done.9
  112.5 1.3 copy-done.6
  113.8 9.3 %crps.1 = bf16[8,352,128]{2,1,0:T(8,128)(2,1)S(1)} custom-call(s32[1]{0:T(128)} %bitcast.member_ref, s32[24,128]{1,0:T(8,128)S(1)} %get-tuple-element.9.ids_ref, bf16[2048,128]{1,0:T(8,128)(2,1)S(1)} %bitcast.19, bf16[2048,128]{1,0:T(8,128)(2,1)S(1)} %collective-permute-done.2.other_ref, bf16[8,16,3072]{2,1,0:T(8,128)(2,1)S(1)} %all-to-all-done.1.behind_ref.parts_ref, ...), custom_call_target="tpu_custom_call" | custom-call | flops 5000000000 | bytes 6000000 | tf_op jit(solution)/shard_map/crps/pallas_call | solution.py:382
  123.1 24.6 %all_to_all.28.got_ref = bf16[8,352,128]{2,1,0:T(8,128)(2,1)S(1)} all-to-all(bf16[8,352,128]{2,1,0:T(8,128)(2,1)S(1)} %crps.1), channel_id=1, replica_groups=mesh['ens'=8,'space'=32] {'ens'}, dimensions={0} | all-to-all | bytes 1441792 | tf_op jit(solution)/shard_map/all_to_all | solution.py:407
  147.6 1.2 unpack.1
  (3 shorter events, 0.0 us)
Async XLA Ops:
  0.6 1.1 copy-start
  1.7 0.7 copy-start.1
  2.4 0.7 copy-start.2
  38.4 9.3 %copy-start.7 = (bf16[128,1024]{1,0:T(8,128)(2,1)S(1)}, bf16[128,1024]{1,0:T(8,128)(2,1)}, u32[]{:S(2)}) copy-start(bf16[128,1024]{1,0:T(8,128)(2,1)} %latent_ref.1) | copy-start | bytes 786436
  38.4 9.3 %copy-start.8 = (bf16[100,1024]{1,0:T(8,128)(2,1)S(1)}, bf16[100,1024]{1,0:T(8,128)(2,1)}, u32[]{:S(2)}) copy-start(bf16[100,1024]{1,0:T(8,128)(2,1)} %embed_ref.1) | copy-start | bytes 614404
  38.4 9.3 %copy-start.10 = (f32[1024]{0:T(1024)S(1)}, f32[1024]{0:T(1024)}, u32[]{:S(2)}) copy-start(f32[1024]{0:T(1024)} %param.18) | copy-start | bytes 12292
  39.5 31.9 %all-to-all-start.1 = ((bf16[8,16,3072]{2,1,0:T(8,128)(2,1)}), bf16[8,16,3072]{2,1,0:T(8,128)(2,1)S(1)}, u32[]{:S(2)}, u32[]{:S(2)}) async-start(bf16[8,16,3072]{2,1,0:T(8,128)(2,1)} %spread.1), calls=%async_computation.1 | async-start | bytes 1572864 | tf_op jit(solution)/shard_map/all_to_all | solution.py:325
  47.7 1.6 %copy-start.3 = (bf16[1024,1024]{1,0:T(8,128)(2,1)S(1)}, bf16[1024,1024]{1,0:T(8,128)(2,1)}, u32[]{:S(2)}) copy-start(bf16[1024,1024]{1,0:T(8,128)(2,1)} %receiver_ref.1) | copy-start | bytes 6291460
  49.3 1.6 %copy-start.4 = (bf16[1024,1024]{1,0:T(8,128)(2,1)S(1)}, bf16[1024,1024]{1,0:T(8,128)(2,1)}, u32[]{:S(2)}) copy-start(bf16[1024,1024]{1,0:T(8,128)(2,1)} %sender_ref.1) | copy-start | bytes 6291460
  50.9 13.2 %copy-start.13 = (s32[128,16]{0,1:T(8,128)S(1)}, s32[128,16]{0,1:T(8,128)}, u32[]{:S(2)}) copy-start(s32[128,16]{0,1:T(8,128)} %param.16) | copy-start | bytes 24580
  61.3 0.8 copy-start.11
  62.1 6.1 %collective-permute-start.1 = (bf16[128,1024]{1,0:T(8,128)(2,1)S(1)}, bf16[128,1024]{1,0:T(8,128)(2,1)S(1)}, u32[]{:S(2)}, u32[]{:S(2)}) collective-permute-start(bf16[128,1024]{1,0:T(8,128)(2,1)S(1)} %get-tuple-element.13.own_ref), channel_id=1, source_target_pairs={{0,31},{1,2},{2,1},{3,4},{4,3},{5,6},{6,5},{7,8},{8,7},{9,10},{10,... | collective-permute-start | bytes 786440 | tf_op jit(solution)/shard_map/ppermute | solution.py:350
  62.5 5.7 %collective-permute-start = (bf16[128,1024]{1,0:T(8,128)(2,1)S(1)}, bf16[128,1024]{1,0:T(8,128)(2,1)S(1)}, u32[]{:S(2)}, u32[]{:S(2)}) collective-permute-start(bf16[128,1024]{1,0:T(8,128)(2,1)S(1)} %get-tuple-element.13.own_ref), channel_id=1, source_target_pairs={{0,1},{1,0},{2,3},{3,2},{4,5},{5,4},{6,7},{7,6},{8,9},{9,8},{10,11... | collective-permute-start | bytes 786440 | tf_op jit(solution)/shard_map/ppermute | solution.py:349
  71.4 1.6 %copy-start.5 = (bf16[1024,1024]{1,0:T(8,128)(2,1)S(1)}, bf16[1024,1024]{1,0:T(8,128)(2,1)}, u32[]{:S(2)}) copy-start(bf16[1024,1024]{1,0:T(8,128)(2,1)} %link_ref.1) | copy-start | bytes 6291460
  73.0 1.0 copy-start.12
  82.2 30.2 %copy-start.9 = (f32[3072]{0:T(1024)S(1)}, f32[3072]{0:T(1024)}, u32[]{:S(2)}) copy-start(f32[3072]{0:T(1024)} %param.25) | copy-start | bytes 36868
  107.3 5.1 %collective-permute-start.2 = (bf16[2048,128]{1,0:T(8,128)(2,1)S(1)}, bf16[2048,128]{1,0:T(8,128)(2,1)S(1)}, u32[]{:S(2)}, u32[]{:S(2)}) collective-permute-start(bf16[2048,128]{1,0:T(8,128)(2,1)S(1)} %bitcast.18), channel_id=1, source_target_pairs={{0,1},{1,0},{2,3},{3,2},{4,5},{5,4},{6,7},{7,6},{8,9},{9,8},{10,11... | collective-permute-start | bytes 1572872 | tf_op jit(solution)/shard_map/ppermute | solution.py:380
  112.5 1.3 copy-start.6
where the time goes:
time: 149 us
  blocking collectives  80.7 us (54%)
  Pallas kernels  34.1 us (23%)
  starting transfers between devices  13.8 us (9%)
  local copies, waits for them, and re-layouts  11.8 us (8%)
  waiting for transfers between devices  7.49 us (5%)
    all_to_all x1, blocking collectives, local(): lax.all_to_all(slots.reshape(spaces, SLOTS, LANE), 'space', split_axis=0,...  31.2 us
    all_to_all x1, blocking collectives, local(): lax.all_to_all(slopes, 'ens', split_axis=0, concat_axis=0, tiled=True)  24.6 us
    all_to_all x1, blocking collectives, local(): lax.all_to_all(jnp.broadcast_to(decoded[None], (spaces // 2, nodes, membe...  15 us
    unnamed x30, local copies, waits for them, and re-layouts  11.6 us
    pallas_call x1, Pallas kernels, local(): pl.pallas_call(encode_kernel, out_shape=(shape((nodes, width), BF16), sha...  10.3 us
    all_to_all x1, blocking collectives, local(): lax.all_to_all(decoded, 'ens', split_axis=0, concat_axis=0, tiled=True)  9.81 us
    pallas_call x1, Pallas kernels, local(): pl.pallas_call(crps_kernel, out_shape=shape((members, rows, LANE), BF16),...  9.29 us
    pallas_call x1, Pallas kernels, local(): pl.pallas_call(process_kernel, out_shape=shape((members, PAD, nodes), BF1...  8.21 us
  transfers between devices with their start and end apart: 4, of which 3 were waited for; matrix products, arithmetic and copies ran while one was open for 1% of the time, Pallas kernels for 7%

commit v1 on v0

v1 whole, which is shorter than its diff:
```python
import functools

import jax
import jax.numpy as jnp
from jax import lax
from jax.experimental import pallas as pl
from jax.experimental.pallas import tpu as pltpu
from jax.sharding import PartitionSpec as P

SLOTS = 192
LANE = 128
SENT = 160
PART = 13
PAD = 16
BF16, F32 = jnp.bfloat16, jnp.float32
VM = pl.BlockSpec(memory_space=pltpu.VMEM)
SM = pl.BlockSpec(memory_space=pltpu.SMEM)


HBM = pl.BlockSpec(memory_space=pltpu.HBM)


def cost(flops, moved, transcendentals=0):
    return pl.CostEstimate(flops=int(flops), bytes_accessed=int(moved), transcendentals=int(transcendentals))


def stay(array):
    return pltpu.with_memory_space_constraint(array, pltpu.HBM)


def params(mib):
    return pltpu.CompilerParams(vmem_limit_bytes=mib * 2**20)


def pack_kernel(
    core_ref, own_hbm, owner_hbm, local_hbm, slots_ref, ids_ref, parts_ref, own_ref, owner_ref, local_ref, wide, rows, slots, pos_v, pos_s, sems
):
    loads = [
        pltpu.make_async_copy(owner_hbm, owner_ref, sems.at[0]),
        pltpu.make_async_copy(local_hbm, local_ref, sems.at[1]),
        pltpu.make_async_copy(own_hbm, own_ref, sems.at[2]),
    ]
    for load in loads:
        load.start()
    slots[...] = jnp.zeros_like(slots)
    loads[0].wait()
    loads[1].wait()
    variables = own_ref.shape[0]
    blocks = owner_ref.shape[0]
    spaces = slots.shape[0] // SLOTS
    row = lax.broadcasted_iota(jnp.int32, (LANE, 2 * LANE), 0)
    col = lax.broadcasted_iota(jnp.int32, (LANE, 2 * LANE), 1)
    before = jnp.where((row < col) | (col >= LANE), 1.0, 0.0).astype(BF16)
    names = lax.broadcasted_iota(jnp.int32, (spaces, LANE), 0)
    carry = jnp.zeros((spaces, LANE), F32)
    for j in range(blocks):
        owner = owner_ref[j : j + 1, :]
        hot = jnp.where(names == owner, 1.0, 0.0)
        counts = jnp.dot(hot.astype(BF16), before, preferred_element_type=F32)
        rank = jnp.sum(hot * (counts[:, :LANE] + carry), axis=0, keepdims=True)
        carry = carry + counts[:, LANE:]
        pos_v[j : j + 1, :] = owner * SLOTS + rank.astype(jnp.int32)
    side = jnp.where(owner_ref[...] % 2 == core_ref[0], 0, spaces // 2)
    ids_ref[...] = (side + owner_ref[...] // 2) * LANE + local_ref[...]
    copy = pltpu.make_async_copy(pos_v, pos_s, sems.at[3])
    copy.start()
    loads[2].wait()
    wide[variables:, :] = jnp.zeros((LANE - variables, wide.shape[1]), F32)
    wide[:variables, :] = own_ref[...].astype(F32)
    for c in range(parts_ref.shape[0]):
        held = min(PART, variables - c * PART)
        piece = wide[c * PART : c * PART + held, :]
        parts_ref[c] = jnp.concatenate([piece, jnp.zeros((PAD - held, wide.shape[1]), F32)], axis=0).astype(BF16)
    for j in range(blocks):
        wide[variables : variables + 1, j * LANE : (j + 1) * LANE] = local_ref[j : j + 1, :].astype(F32)
    for j in range(blocks):
        rows[j * LANE : (j + 1) * LANE, :] = wide[:, j * LANE : (j + 1) * LANE].T
    copy.wait()

    def place(j, _):
        for i in range(0, LANE, 16):
            base = pl.multiple_of(j * LANE + i, 16)
            held = [rows[pl.ds(base + k, 1), :] for k in range(16)]
            for k in range(16):
                slots[pl.ds(pos_s[j, i + k], 1), :] = held[k]
        return 0

    lax.fori_loop(0, blocks, place, 0)
    used = variables + 1
    spare = LANE - used
    more = SLOTS - SENT
    lanes = lax.broadcasted_iota(jnp.int32, (more, LANE), 1)
    for o in range(spaces):
        beyond = slots[o * SLOTS + SENT : (o + 1) * SLOTS, :]
        for p in range(SENT // more):
            piece = slots[o * SLOTS + p * more : o * SLOTS + (p + 1) * more, :]
            if p * spare < used:
                piece = jnp.where(lanes >= used, pltpu.roll(beyond, used - p * spare, 1), piece)
            slots_ref[o * SENT + p * more : o * SENT + (p + 1) * more, :] = piece.astype(BF16)


def encode_kernel(
    slots_ref,
    embed_ref,
    latent_ref,
    gain_ref,
    sender_ref,
    normed_ref,
    source_ref,
    beyond,
    sender,
    sem,
):
    copy = pltpu.make_async_copy(sender_ref, sender, sem)
    copy.start()
    variables = embed_ref.shape[0]
    width = embed_ref.shape[1]
    chunk = 512
    half = jnp.concatenate([embed_ref[...].astype(F32) * 0.5, jnp.zeros((LANE - variables, width), F32)], axis=0).astype(BF16)
    lanes = lax.broadcasted_iota(jnp.int32, (chunk, LANE), 1).astype(F32)
    state = latent_ref[...].astype(F32)
    used = variables + 1
    spare = LANE - used
    more = SLOTS - SENT
    place = lax.broadcasted_iota(jnp.int32, (more, LANE), 1)
    for o in range(slots_ref.shape[0] // SENT):
        whole = jnp.zeros((more, LANE), F32)
        for p in range(-(-used // spare)):
            piece = slots_ref[o * SENT + p * more : o * SENT + (p + 1) * more, :].astype(F32)
            there = (place >= p * spare) & (place < (p + 1) * spare)
            whole = jnp.where(there, pltpu.roll(piece, (p * spare - used) % LANE, 1), whole)
        beyond[o * more : (o + 1) * more, :] = whole.astype(BF16)
    whole = slots_ref.shape[0] // chunk
    for c in range(whole + beyond.shape[0] // chunk):
        if c < whole:
            x = slots_ref[c * chunk : (c + 1) * chunk, :]
        else:
            x = beyond[(c - whole) * chunk : (c - whole + 1) * chunk, :]
        h = jnp.dot(x, half, preferred_element_type=F32)
        act = (h + h * jnp.tanh(h)).astype(BF16)
        node = x[:, variables : variables + 1].astype(F32)
        hot = jnp.where(node == lanes, 1.0, 0.0).astype(BF16)
        state = state + lax.dot_general(hot, act, (((0,), (0,)), ((), ())), preferred_element_type=F32)
    centred = state - jnp.mean(state, axis=-1, keepdims=True)
    spread = jnp.mean(centred * centred, axis=-1, keepdims=True)
    normed = (centred * lax.rsqrt(spread + 1e-05) * gain_ref[...]).astype(BF16)
    normed_ref[...] = normed
    copy.wait()
    source_ref[...] = jnp.dot(normed, sender[...], preferred_element_type=F32).astype(BF16)


def near_kernel(
    member_ref,
    near_ref,
    normed_ref,
    sibling_ref,
    own_ref,
    receiver_hbm,
    observed_hbm,
    half_ref,
    seen_ref,
    receiver,
    observed,
    beside,
    sems,
):
    loads = [
        pltpu.make_async_copy(receiver_hbm, receiver, sems.at[0]),
        pltpu.make_async_copy(observed_hbm, observed, sems.at[1]),
    ]
    for load in loads:
        load.start()
    nodes, fanout = near_ref.shape
    group = 4
    beside[:nodes, :] = sibling_ref[...]
    beside[nodes:, :] = own_ref[...]
    lanes = lax.broadcasted_iota(jnp.int32, (nodes, 2 * nodes), 1)
    loads[0].wait()
    query = 0.5 * jnp.dot(normed_ref[...], receiver[...], preferred_element_type=F32)
    for g in range(0, fanout, group):
        hot = jnp.concatenate(
            [jnp.where(near_ref[:, k : k + 1] == lanes, 0.5, 0.0) for k in range(g, g + group)], axis=0
        ).astype(BF16)
        picked = jnp.dot(hot, beside[...], preferred_element_type=F32)
        half_ref[g * nodes : (g + group) * nodes, :] = picked + jnp.concatenate([query] * group, axis=0)
    loads[1].wait()
    variables = observed.shape[0]
    for c in range(-(-variables // PART)):

        @pl.when(member_ref[0] == c)
        def _():
            count = min(PART, variables - c * PART)
            seen_ref[...] = jnp.zeros_like(seen_ref)
            seen_ref[:count, :] = observed[c * PART : c * PART + count, :]


def process_kernel(
    near_ref, half_ref, normed_ref, other_ref, link_ref, decode_ref, out_ref, edges, total, spaced, link, sem
):
    copy = pltpu.make_async_copy(link_ref, link, sem)
    copy.start()
    nodes, fanout = near_ref.shape
    variables = decode_ref.shape[0]
    group = 4
    lanes = lax.broadcasted_iota(jnp.int32, (nodes, nodes), 1) + 2 * nodes
    for g in range(0, fanout, group):
        hot = jnp.concatenate(
            [jnp.where(near_ref[:, k : k + 1] == lanes, 0.5, 0.0) for k in range(g, g + group)], axis=0
        ).astype(BF16)
        h = half_ref[g * nodes : (g + group) * nodes, :] + jnp.dot(hot, other_ref[...], preferred_element_type=F32)
        edges[g * nodes : (g + group) * nodes, :] = (h + h * jnp.tanh(h)).astype(BF16)
    copy.wait()
    for g in range(0, fanout, group):
        z = jnp.dot(edges[g * nodes : (g + group) * nodes, :], link[...], preferred_element_type=F32)
        z = z + z * jnp.tanh(0.5 * z)
        part = sum(z[k * nodes : (k + 1) * nodes] for k in range(group))
        if g == 0:
            total[...] = part
        else:
            total[...] += part
    updated = (normed_ref[...].astype(F32) + total[...] * (0.5 / fanout)).astype(BF16)
    decoded = lax.dot_general(decode_ref[...], updated, (((1,), (1,)), ((), ())), preferred_element_type=F32)
    spaced[...] = jnp.zeros_like(spaced)
    for c in range(out_ref.shape[0]):
        held = min(PART, variables - c * PART)
        spaced[c * PAD : c * PAD + held, :] = decoded[c * PART : c * PART + held, :]
    for c in range(out_ref.shape[0]):
        out_ref[c] = spaced[c * PAD : (c + 1) * PAD, :].astype(BF16)


def crps_kernel(ids_ref, table_ref, other_ref, parts_ref, seen, area_ref, out_ref, table, slopes, picked, held):
    members = parts_ref.shape[0]
    blocks = ids_ref.shape[0]
    per_member = blocks // members
    rows = out_ref.shape[1]
    half = table_ref.shape[0]
    table[:half, :] = table_ref[...].astype(F32)
    table[half:, :] = other_ref[...].astype(F32)
    for m in range(members):
        slopes[m * rows + rows - 8 : (m + 1) * rows, :] = jnp.zeros((8, LANE), F32)
    def fetch(j, turn):
        for i in range(0, LANE, 16):
            row = [table[pl.ds(ids_ref[j, i + k], 1), :] for k in range(16)]
            for k in range(16):
                picked[turn * LANE + i + k : turn * LANE + i + k + 1, :] = row[k]

    def score(j, turn):
        here = pl.ds(pl.multiple_of(j * LANE, LANE), LANE)
        held[turn * LANE : (turn + 1) * LANE, :] = picked[turn * LANE : (turn + 1) * LANE, :].T
        area = area_ref[pl.ds(j, 1), :]
        spare = j // per_member * rows + PART * blocks + j % per_member
        for low in range(0, PAD, 8):
            count = min(8, PART - low)
            start = turn * LANE + low
            f = [
                held[start + m * PAD : start + m * PAD + 8, :] + parts_ref[m, :, here][low : low + 8].astype(F32)
                for m in range(members)
            ]
            obs = seen[low : low + 8, here]
            slope = [None] * members
            pairs = None
            for a in range(members):
                for b in range(a + 1, members):
                    d = f[a] - f[b]
                    q = d * d + 0.01
                    r = lax.rsqrt(q)
                    t = d * r
                    pairs = q * r if pairs is None else pairs + q * r
                    slope[a] = t if slope[a] is None else slope[a] + t
                    slope[b] = -t if slope[b] is None else slope[b] - t
            near = None
            for m in range(members):
                miss = f[m] - obs
                q = miss * miss + 0.01
                r = lax.rsqrt(q)
                near = q * r if near is None else near + q * r
                value = area * (miss * r - slope[m] * (1.0 / (members - 1)))
                slopes[pl.ds(m * rows + low * blocks + j, count, stride=blocks), :] = value[:count]
            pairs = (2.0 * pairs + 0.1 * members) * (1.0 / (2.0 * members * (members - 1)))
            value = area * (near * (1.0 / members) - pairs)
            slopes[pl.ds(spare + low * per_member, count, stride=per_member), :] = value[:count]

    fetch(0, 0)

    def two(i, _):
        fetch(2 * i + 1, 1)
        score(2 * i, 0)
        fetch(jnp.minimum(2 * i + 2, blocks - 1), 0)
        score(2 * i + 1, 1)
        return 0

    lax.fori_loop(0, blocks // 2, two, 0)
    for m in range(members):
        out_ref[m] = slopes[m * rows : (m + 1) * rows, :].astype(BF16)


def unpack_kernel(got_ref, crps_ref, grads_ref, wide):
    variables, points = crps_ref.shape
    parts = got_ref.shape[0]
    per_part = points // LANE
    blocks = parts * per_part
    for c in range(parts):
        wide[...] = got_ref[c].astype(F32)
        held = min(PART, variables - c * PART)
        grads_ref[c * PART * blocks : (c * PART + held) * blocks, :] = wide[: held * blocks, :]
        for j in range(per_part):
            crps_ref[c * PART : c * PART + held, j * LANE : (j + 1) * LANE] = wide[
                pl.ds(PART * blocks + j, held, stride=per_part), :
            ]


def local(
    initial_states,
    owner,
    node_local,
    adjacent_vertex_ids,
    vertex_latents,
    norm_factor,
    grid_to_mesh_matrix,
    receiver_matrix,
    sender_matrix,
    link_update_matrix,
    mesh_to_grid_matrix,
    observed,
    area,
):
    spaces = lax.axis_size("space")
    members = lax.axis_size("ens")
    variables, points = initial_states.shape[1:]
    nodes, width = vertex_latents.shape
    fanout = adjacent_vertex_ids.shape[1]
    blocks = points // LANE
    shape = jax.ShapeDtypeStruct
    place = lax.axis_index("space")
    core = place % 2
    slots, ids, parts = pl.pallas_call(
        pack_kernel,
        out_shape=(
            shape((spaces * SENT, LANE), BF16),
            shape((blocks, LANE), jnp.int32),
            shape((members, PAD, points), BF16),
        ),
        in_specs=[SM] + [HBM] * 3,
        out_specs=(VM,) * 3,
        scratch_shapes=[
            pltpu.VMEM((variables, points), BF16),
            pltpu.VMEM((blocks, LANE), jnp.int32),
            pltpu.VMEM((blocks, LANE), jnp.int32),
            pltpu.VMEM((LANE, points), F32),
            pltpu.VMEM((points, LANE), F32),
            pltpu.VMEM((spaces * SLOTS, LANE), F32),
            pltpu.VMEM((blocks, LANE), jnp.int32),
            pltpu.SMEM((blocks, LANE), jnp.int32),
            pltpu.SemaphoreType.DMA((4,)),
        ],
        compiler_params=params(16),
        cost_estimate=cost(1.5e8, 8e6),
        name="pack",
    )(
        core.astype(jnp.int32).reshape(1),
        stay(initial_states[0]),
        stay(owner.reshape(blocks, LANE)),
        stay(node_local.reshape(blocks, LANE)),
    )
    got = lax.all_to_all(slots.reshape(spaces, SENT, LANE), "space", split_axis=0, concat_axis=0, tiled=True)
    got, parts = lax.optimization_barrier((got, parts))
    parts = lax.all_to_all(parts, "ens", split_axis=0, concat_axis=0, tiled=True)
    normed, source = pl.pallas_call(
        encode_kernel,
        out_shape=(shape((nodes, width), BF16), shape((nodes, width), BF16)),
        in_specs=[VM] * 4 + [HBM],
        out_specs=(VM,) * 2,
        scratch_shapes=[
            pltpu.VMEM((spaces * (SLOTS - SENT), LANE), BF16),
            pltpu.VMEM((width, width), BF16),
            pltpu.SemaphoreType.DMA,
        ],
        compiler_params=params(20),
        cost_estimate=cost(4e9, 8e6, 6.3e6),
        name="encode",
    )(
        got.reshape(spaces * SENT, LANE),
        grid_to_mesh_matrix,
        vertex_latents,
        norm_factor.reshape(1, width),
        stay(sender_matrix),
    )
    sibling = lax.ppermute(source, "space", [(i, i ^ 1) for i in range(spaces)])
    other = lax.ppermute(source, "space", [(i, (i + 2 * (i % 2) - 1) % spaces) for i in range(spaces)])
    home = adjacent_vertex_ids // nodes
    slab = jnp.where(home == place, 1, jnp.where(home == place + 1 - 2 * core, 0, 2))
    near = slab * nodes + adjacent_vertex_ids % nodes
    half, seen = pl.pallas_call(
        near_kernel,
        out_shape=(shape((fanout * nodes, width), F32), shape((PAD, points), F32)),
        in_specs=[SM] + [VM] * 4 + [HBM] * 2,
        out_specs=(VM, VM),
        scratch_shapes=[
            pltpu.VMEM((width, width), BF16),
            pltpu.VMEM((variables, points), F32),
            pltpu.VMEM((2 * nodes, width), BF16),
            pltpu.SemaphoreType.DMA((2,)),
        ],
        compiler_params=params(16),
        cost_estimate=cost(2e9, 4e6),
        name="near",
    )(
        lax.axis_index("ens").astype(jnp.int32).reshape(1),
        near,
        normed,
        sibling,
        source,
        stay(receiver_matrix),
        stay(observed),
    )
    decoded = pl.pallas_call(
        process_kernel,
        out_shape=shape((members, PAD, nodes), BF16),
        in_specs=[VM] * 4 + [HBM, VM],
        out_specs=VM,
        scratch_shapes=[
            pltpu.VMEM((fanout * nodes, width), BF16),
            pltpu.VMEM((nodes, width), F32),
            pltpu.VMEM((members * PAD, nodes), F32),
            pltpu.VMEM((width, width), BF16),
            pltpu.SemaphoreType.DMA,
        ],
        compiler_params=params(20),
        cost_estimate=cost(6e9, 4e6, 4.2e6),
        name="process",
    )(near, half, normed, other, stay(link_update_matrix), mesh_to_grid_matrix.T)
    decoded, parts = lax.optimization_barrier((decoded, parts))
    decoded = lax.all_to_all(decoded, "ens", split_axis=0, concat_axis=0, tiled=True)
    decoded = decoded.reshape(members * PAD, nodes).T
    table = lax.all_to_all(
        jnp.broadcast_to(decoded[None], (spaces // 2, nodes, members * PAD)),
        "space",
        split_axis=0,
        concat_axis=0,
        tiled=True,
        axis_index_groups=[list(range(c, spaces, 2)) for c in range(2)],
    ).reshape(spaces // 2 * nodes, members * PAD)
    table_other = lax.ppermute(table, "space", [(i, i ^ 1) for i in range(spaces)])
    rows = -(-PART * (blocks + blocks // members) // 16) * 16
    slopes = pl.pallas_call(
        crps_kernel,
        out_shape=shape((members, rows, LANE), BF16),
        in_specs=[SM] + [VM] * 5,
        out_specs=VM,
        scratch_shapes=[
            pltpu.VMEM((spaces * nodes, LANE), F32),
            pltpu.VMEM((members * rows, LANE), F32),
            pltpu.VMEM((2 * LANE, LANE), F32),
            pltpu.VMEM((2 * members * PAD, LANE), F32),
        ],
        compiler_params=params(20),
        cost_estimate=cost(5e9, 6e6, 2e6),
        name="crps",
    )(
        ids,
        table,
        table_other,
        parts,
        seen,
        area.reshape(blocks, LANE),
    )
    slopes = lax.all_to_all(slopes, "ens", split_axis=0, concat_axis=0, tiled=True)
    crps, grads = pl.pallas_call(
        unpack_kernel,
        out_shape=(shape((variables, points // members), F32), shape((variables * blocks, LANE), F32)),
        in_specs=[VM],
        out_specs=(VM, VM),
        scratch_shapes=[pltpu.VMEM((rows, LANE), F32)],
        compiler_params=params(16),
        cost_estimate=cost(1e6, 2e6),
        name="unpack",
    )(slopes)
    return crps, grads.reshape(1, variables, points)


def solution(mesh):
    return jax.shard_map(
        local,
        mesh=mesh,
        in_specs=(
            P("ens", None, "space"),
            P("space", None),
            P("space"),
            P("space", None),
            P("space", None),
            P(),
            P(),
            P(),
            P(),
            P(),
            P(),
            P(None, "space"),
            P("space"),
        ),
        out_specs=(P(None, ("space", "ens")), P("ens", None, "space")),
        check_vma=False,
    )
```

time: 149 us -> 131 us (0.88)
  local copies, waits for them, and re-layouts: 11.8 us -> 0.35 us
  Pallas kernels: 34.1 us -> 31.9 us
  waiting for transfers between devices: 7.49 us -> 5.51 us
    unnamed x30 -> x13, local copies, waits for them, and re-layouts: 11.6 us -> 0.13 us
    pallas_call x2, Pallas kernels: 5.13 us -> 9.01 us  [the longest x1 5.54 us: local(): pl.pallas_call(pack_kernel, out_shape=(shape((spaces * SENT, LANE), BF16)...]
    pallas_call x1, Pallas kernels: 9.29 us -> 6.55 us  [local(): pl.pallas_call(crps_kernel, out_shape=shape((members, rows, LANE), BF16),...]
    all_to_all x1, blocking collectives: 31.2 us -> 28.7 us  [local(): lax.all_to_all(slots.reshape(spaces, SENT, LANE), 'space', split_axis=0,...]
    all_to_all x1, blocking collectives: 9.81 us -> 12 us  [local(): lax.all_to_all(decoded, 'ens', split_axis=0, concat_axis=0, tiled=True)]
    pallas_call x1, Pallas kernels: 10.3 us -> 8.42 us  [local(): pl.pallas_call(encode_kernel, out_shape=(shape((nodes, width), BF16), sha...]
    all_to_all x1, waiting for transfers between devices: 3.21 us -> 1.58 us  [local(): lax.all_to_all(parts, 'ens', split_axis=0, concat_axis=0, tiled=True)]
  transfers between devices with their start and end apart: 4 -> 4, of which waited for: 3 -> 4; matrix products, arithmetic and copies ran while one was open for 1% -> 0% of each run, Pallas kernels for 7% -> 14%
where the time goes in v1:
time: 131 us
  blocking collectives  79.8 us (61%)
  Pallas kernels  31.9 us (24%)
  starting transfers between devices  12.5 us (10%)
  waiting for transfers between devices  5.51 us (4%)
    all_to_all x1, blocking collectives, local(): lax.all_to_all(slots.reshape(spaces, SENT, LANE), 'space', split_axis=0,...  28.7 us
    all_to_all x1, blocking collectives, local(): lax.all_to_all(slopes, 'ens', split_axis=0, concat_axis=0, tiled=True)  24.6 us
    all_to_all x1, blocking collectives, local(): lax.all_to_all(jnp.broadcast_to(decoded[None], (spaces // 2, nodes, membe...  14.5 us
    all_to_all x1, blocking collectives, local(): lax.all_to_all(decoded, 'ens', split_axis=0, concat_axis=0, tiled=True)  12 us
    pallas_call x1, Pallas kernels, local(): pl.pallas_call(encode_kernel, out_shape=(shape((nodes, width), BF16), sha...  8.42 us
    all_to_all x1, starting transfers between devices, local(): lax.all_to_all(parts, 'ens', split_axis=0, concat_axis=0, tiled=True)  8.18 us
    pallas_call x1, Pallas kernels, local(): pl.pallas_call(process_kernel, out_shape=shape((members, PAD, nodes), BF1...  6.74 us
    pallas_call x1, Pallas kernels, local(): pl.pallas_call(crps_kernel, out_shape=shape((members, rows, LANE), BF16),...  6.55 us
  transfers between devices with their start and end apart: 4, of which 4 were waited for; matrix products, arithmetic and copies ran while one was open for 0% of the time, Pallas kernels for 14%

profile of v1, /device:TPU:1, one launch (start us, length us, event | category | flops | bytes accessed | tf_op | source)
XLA Modules:
  0.0 130.9 jit_solution(5776611830876263914)
XLA Ops:
  0.6 5.5 %pack.1 = (bf16[5120,128]{1,0:T(8,128)(2,1)S(1)}, s32[24,128]{1,0:T(8,128)S(1)}, bf16[8,16,3072]{2,1,0:T(8,128)(2,1)}) custom-call(s32[1]{0:T(128)} %bitcast.core_ref, bf16[100,3072]{1,0:T(8,128)(2,1)} %bitcast.22, s32[24,128]{1,0:T(8,128)} %bitcast.24, s32[24,128]{1,0:T(8,128)} %bitcast.25), custom_call_target="tpu_custom_call" | custom-call | flops 150000000 | bytes 8000000 | tf_op jit(solution)/shard_map/pack/pallas_call | solution.py:336
  6.2 0.0 copy-start
  6.2 0.0 copy-start.1
  6.2 0.0 copy-start.4
  6.2 28.7 %all_to_all.25 = bf16[32,160,128]{2,1,0:T(8,128)(2,1)S(1)} all-to-all(bf16[32,160,128]{2,1,0:T(8,128)(2,1)S(1)} %bitcast.16), channel_id=1, replica_groups=mesh['ens'=8,'space'=32] {'space'}, dimensions={0} | all-to-all | bytes 2621440 | tf_op jit(solution)/shard_map/all_to_all | solution.py:365
  35.0 8.2 %all-to-all-start.1 = ((bf16[8,16,3072]{2,1,0:T(8,128)(2,1)}), bf16[8,16,3072]{2,1,0:T(8,128)(2,1)S(1)}, u32[]{:S(2)}, u32[]{:S(2)}) async-start(bf16[8,16,3072]{2,1,0:T(8,128)(2,1)} %get-tuple-element.22), calls=%async_computation.1 | async-start | bytes 1572864 | tf_op jit(solution)/shard_map/all_to_all | solution.py:367
  43.2 0.0 copy-done
  43.2 0.0 copy-done.1
  43.2 0.0 copy-done.4
  43.2 0.0 copy-start.5
  43.2 8.4 %encode.1 = (bf16[128,1024]{1,0:T(8,128)(2,1)S(1)}, bf16[128,1024]{1,0:T(8,128)(2,1)S(1)}) custom-call(bf16[5120,128]{1,0:T(8,128)(2,1)S(1)} %bitcast.15, bf16[100,1024]{1,0:T(8,128)(2,1)S(1)} %copy-done.1, bf16[128,1024]{1,0:T(8,128)(2,1)S(1)} %copy-done, f32[1,1024]{1,0:T(1,128)S(1)} %bitcast.21, bf16[1024,1024]{1,0:T(8,128)(2,1)} %sender_ref.1), custom_call_target="tpu_custom_call" | custom-call | flops 4000000000 | bytes 8000000 | tf_op jit(solution)/shard_map/encode/pallas_call | solution.py:368
  51.6 0.6 collective-permute-start
  52.2 0.0 copy-done.5
  52.2 0.1 copy.21
  52.3 0.2 collective-permute-start.1
  52.5 0.1 fusion.near_ref
  52.6 0.8 collective-permute-done.sibling_ref
  53.3 0.0 copy-start.2
  53.3 3.5 %near.1 = (f32[2048,1024]{1,0:T(8,128)S(1)}, f32[16,3072]{1,0:T(8,128)S(1)}) custom-call(s32[1]{0:T(128)} %bitcast.4.member_ref, s32[128,16]{1,0:T(8,128)S(1)} %fusion.near_ref, bf16[128,1024]{1,0:T(8,128)(2,1)S(1)} %get-tuple-element.19.normed_ref, bf16[128,1024]{1,0:T(8,128)(2,1)S(1)} %collective-permute-done.sibling_ref, ...), custom_call_target="tpu_custom_call" | custom-call | flops 2000000000 | bytes 4000000 | tf_op jit(solution)/shard_map/near/pallas_call | solution.py:393
  56.8 1.6 %collective-permute-done.1.other_ref = bf16[128,1024]{1,0:T(8,128)(2,1)S(1)} collective-permute-done((bf16[128,1024]{1,0:T(8,128)(2,1)S(1)}, bf16[128,1024]{1,0:T(8,128)(2,1)S(1)}, u32[]{:S(2)}, u32[]{:S(2)}) %collective-permute-start.1) | collective-permute-done | bytes 262176 | tf_op jit(solution)/shard_map/ppermute | solution.py:389
  58.4 0.0 copy-done.2
  58.5 0.0 copy-start.3
  58.5 6.7 %process.1 = bf16[8,16,128]{2,1,0:T(8,128)(2,1)S(1)} custom-call(s32[128,16]{1,0:T(8,128)S(1)} %fusion.near_ref, f32[2048,1024]{1,0:T(8,128)S(1)} %get-tuple-element.21.half_ref, bf16[128,1024]{1,0:T(8,128)(2,1)S(1)} %get-tuple-element.19.normed_ref, bf16[128,1024]{1,0:T(8,128)(2,1)S(1)} %collective-permute-done.1.other_ref, bf16[1024,1024]{1,0:T(8,128)(2,1)} %link_ref.1, ...), custom_call_target="tpu_custom_call" | custom-call | flops 6000000000 | bytes 4000000 | tf_op jit(solution)/shard_map/process/pallas_call | solution.py:416
  65.2 1.6 %all-to-all-done.1.parts_ref = bf16[8,16,3072]{2,1,0:T(8,128)(2,1)S(1)} async-done(((bf16[8,16,3072]{2,1,0:T(8,128)(2,1)}), bf16[8,16,3072]{2,1,0:T(8,128)(2,1)S(1)}, u32[]{:S(2)}, u32[]{:S(2)}) %all-to-all-start.1) | async-done | bytes 786464 | tf_op jit(solution)/shard_map/all_to_all | solution.py:367
  66.8 12.0 %all_to_all.26 = bf16[8,16,128]{2,1,0:T(8,128)(2,1)S(1)} all-to-all(bf16[8,16,128]{2,1,0:T(8,128)(2,1)S(1)} %process.1), channel_id=1, replica_groups=mesh['ens'=8,'space'=32] {'ens'}, dimensions={0} | all-to-all | bytes 65536 | tf_op jit(solution)/shard_map/all_to_all | solution.py:433
  78.8 0.1 copy.25
  78.9 0.1 broadcast_in_dim.15
  79.0 14.5 %all_to_all.27 = bf16[16,128,128]{2,1,0:T(8,128)(2,1)S(1)} all-to-all(bf16[16,128,128]{2,1,0:T(8,128)(2,1)S(1)} %broadcast_in_dim.15), channel_id=1, replica_groups={{0,2,4,6,8,10,12,14,16,18,20,22,24,26,28,30},{1,3,5,7,9,11,13,15,17,19,..., dimensions={0} | all-to-all | bytes 1048576 | tf_op jit(solution)/shard_map/all_to_all | solution.py:435
  93.5 3.6 %collective-permute-start.2 = (bf16[2048,128]{1,0:T(8,128)(2,1)S(1)}, bf16[2048,128]{1,0:T(8,128)(2,1)S(1)}, u32[]{:S(2)}, u32[]{:S(2)}) collective-permute-start(bf16[2048,128]{1,0:T(8,128)(2,1)S(1)} %bitcast.17), channel_id=1, source_target_pairs={{0,1},{1,0},{2,3},{3,2},{4,5},{5,4},{6,7},{7,6},{8,9},{9,8},{10,11... | collective-permute-start | bytes 1572872 | tf_op jit(solution)/shard_map/ppermute | solution.py:443
  97.1 1.5 %collective-permute-done.2.other_ref = bf16[2048,128]{1,0:T(8,128)(2,1)S(1)} collective-permute-done((bf16[2048,128]{1,0:T(8,128)(2,1)S(1)}, bf16[2048,128]{1,0:T(8,128)(2,1)S(1)}, u32[]{:S(2)}, u32[]{:S(2)}) %collective-permute-start.2) | collective-permute-done | bytes 524320 | tf_op jit(solution)/shard_map/ppermute | solution.py:443
  98.6 0.0 copy-done.3
  98.6 6.6 %crps.1 = bf16[8,352,128]{2,1,0:T(8,128)(2,1)S(1)} custom-call(s32[24,128]{1,0:T(8,128)S(1)} %get-tuple-element.15.ids_ref, bf16[2048,128]{1,0:T(8,128)(2,1)S(1)} %bitcast.18, bf16[2048,128]{1,0:T(8,128)(2,1)S(1)} %collective-permute-done.2.other_ref, bf16[8,16,3072]{2,1,0:T(8,128)(2,1)S(1)} %all-to-all-done.1.parts_ref, ...), custom_call_target="tpu_custom_call" | custom-call | flops 5000000000 | bytes 6000000 | tf_op jit(solution)/shard_map/crps/pallas_call | solution.py:445
  105.2 24.6 %all_to_all.28.got_ref = bf16[8,352,128]{2,1,0:T(8,128)(2,1)S(1)} all-to-all(bf16[8,352,128]{2,1,0:T(8,128)(2,1)S(1)} %crps.1), channel_id=1, replica_groups=mesh['ens'=8,'space'=32] {'ens'}, dimensions={0} | all-to-all | bytes 1441792 | tf_op jit(solution)/shard_map/all_to_all | solution.py:467
  129.8 1.2 unpack.1
Async XLA Ops:
  6.2 37.0 %copy-start = (bf16[128,1024]{1,0:T(8,128)(2,1)S(1)}, bf16[128,1024]{1,0:T(8,128)(2,1)}, u32[]{:S(2)}) copy-start(bf16[128,1024]{1,0:T(8,128)(2,1)} %latent_ref.1) | copy-start | bytes 786436
  6.2 37.0 %copy-start.1 = (bf16[100,1024]{1,0:T(8,128)(2,1)S(1)}, bf16[100,1024]{1,0:T(8,128)(2,1)}, u32[]{:S(2)}) copy-start(bf16[100,1024]{1,0:T(8,128)(2,1)} %embed_ref.1) | copy-start | bytes 614404
  6.2 37.0 %copy-start.4 = (f32[1024]{0:T(1024)S(1)}, f32[1024]{0:T(1024)}, u32[]{:S(2)}) copy-start(f32[1024]{0:T(1024)} %param.18) | copy-start | bytes 12292
  35.0 31.8 %all-to-all-start.1 = ((bf16[8,16,3072]{2,1,0:T(8,128)(2,1)}), bf16[8,16,3072]{2,1,0:T(8,128)(2,1)S(1)}, u32[]{:S(2)}, u32[]{:S(2)}) async-start(bf16[8,16,3072]{2,1,0:T(8,128)(2,1)} %get-tuple-element.22), calls=%async_computation.1 | async-start | bytes 1572864 | tf_op jit(solution)/shard_map/all_to_all | solution.py:367
  43.2 9.0 %copy-start.5 = (s32[128,16]{0,1:T(8,128)S(1)}, s32[128,16]{0,1:T(8,128)}, u32[]{:S(2)}) copy-start(s32[128,16]{0,1:T(8,128)} %param.16) | copy-start | bytes 24580
  51.6 1.7 %collective-permute-start = (bf16[128,1024]{1,0:T(8,128)(2,1)S(1)}, bf16[128,1024]{1,0:T(8,128)(2,1)S(1)}, u32[]{:S(2)}, u32[]{:S(2)}) collective-permute-start(bf16[128,1024]{1,0:T(8,128)(2,1)S(1)} %get-tuple-element.20.own_ref), channel_id=1, source_target_pairs={{0,1},{1,0},{2,3},{3,2},{4,5},{5,4},{6,7},{7,6},{8,9},{9,8},{10,11... | collective-permute-start | bytes 786440 | tf_op jit(solution)/shard_map/ppermute | solution.py:388
  52.3 6.2 %collective-permute-start.1 = (bf16[128,1024]{1,0:T(8,128)(2,1)S(1)}, bf16[128,1024]{1,0:T(8,128)(2,1)S(1)}, u32[]{:S(2)}, u32[]{:S(2)}) collective-permute-start(bf16[128,1024]{1,0:T(8,128)(2,1)S(1)} %get-tuple-element.20.own_ref), channel_id=1, source_target_pairs={{0,31},{1,2},{2,1},{3,4},{4,3},{5,6},{6,5},{7,8},{8,7},{9,10},{10,... | collective-permute-start | bytes 786440 | tf_op jit(solution)/shard_map/ppermute | solution.py:389
  53.3 5.1 %copy-start.2 = (bf16[1024,100]{0,1:T(8,128)(2,1)S(1)}, bf16[1024,100]{0,1:T(8,128)(2,1)}, u32[]{:S(2)}) copy-start(bf16[1024,100]{0,1:T(8,128)(2,1)} %param.23) | copy-start | bytes 614404
  58.5 40.2 %copy-start.3 = (f32[3072]{0:T(1024)S(1)}, f32[3072]{0:T(1024)}, u32[]{:S(2)}) copy-start(f32[3072]{0:T(1024)} %param.25) | copy-start | bytes 36868
  93.5 5.1 %collective-permute-start.2 = (bf16[2048,128]{1,0:T(8,128)(2,1)S(1)}, bf16[2048,128]{1,0:T(8,128)(2,1)S(1)}, u32[]{:S(2)}, u32[]{:S(2)}) collective-permute-start(bf16[2048,128]{1,0:T(8,128)(2,1)S(1)} %bitcast.17), channel_id=1, source_target_pairs={{0,1},{1,0},{2,3},{3,2},{4,5},{5,4},{6,7},{7,6},{8,9},{9,8},{10,11... | collective-permute-start | bytes 1572872 | tf_op jit(solution)/shard_map/ppermute | solution.py:443

commit v2 on v1

--- a/solution.py
+++ b/solution.py
@@ -33,8 +33,9 @@
 
 
 def pack_kernel(
-    core_ref, own_hbm, owner_hbm, local_hbm, slots_ref, ids_ref, parts_ref, own_ref, owner_ref, local_ref, wide, rows, slots, pos_v, pos_s, sems
+    core_ref, own_hbm, owner_hbm, local_hbm, slots_ref, ids_ref, *rest
 ):
+    *parts, own_ref, owner_ref, local_ref, wide, rows, slots, flat, pos_v, pos_s, sems = rest
     loads = [
         pltpu.make_async_copy(owner_hbm, owner_ref, sems.at[0]),
         pltpu.make_async_copy(local_hbm, local_ref, sems.at[1]),
@@ -67,10 +68,15 @@
     loads[2].wait()
     wide[variables:, :] = jnp.zeros((LANE - variables, wide.shape[1]), F32)
     wide[:variables, :] = own_ref[...].astype(F32)
-    for c in range(parts_ref.shape[0]):
-        held = min(PART, variables - c * PART)
-        piece = wide[c * PART : c * PART + held, :]
-        parts_ref[c] = jnp.concatenate([piece, jnp.zeros((PAD - held, wide.shape[1]), F32)], axis=0).astype(BF16)
+    members = len(parts)
+    for j in range(blocks):
+        for low in range(0, variables, 8):
+            count = min(8, variables - low)
+            flat[pl.ds(low * blocks + j, count, stride=blocks), :] = wide[low : low + count, j * LANE : (j + 1) * LANE]
+    flat[variables * blocks :, :] = jnp.zeros((flat.shape[0] - variables * blocks, LANE), F32)
+    for d in range(members):
+        first = pl.multiple_of((core_ref[1] + d) % members * (PART * blocks), 8)
+        parts[d][...] = flat[pl.ds(first, parts[d].shape[0]), :].astype(BF16)
     for j in range(blocks):
         wide[variables : variables + 1, j * LANE : (j + 1) * LANE] = local_ref[j : j + 1, :].astype(F32)
     for j in range(blocks):
@@ -228,14 +234,20 @@
         out_ref[c] = spaced[c * PAD : (c + 1) * PAD, :].astype(BF16)
 
 
-def crps_kernel(ids_ref, table_ref, other_ref, parts_ref, seen, area_ref, out_ref, table, slopes, picked, held):
-    members = parts_ref.shape[0]
+def crps_kernel(member_ref, ids_ref, table_ref, other_ref, seen, area_ref, *rest):
+    *parts, out_ref, table, states, slopes, picked, held = rest
+    members = len(parts)
+    names = [(member_ref[0] + members - d) % members for d in range(members)]
     blocks = ids_ref.shape[0]
     per_member = blocks // members
     rows = out_ref.shape[1]
     half = table_ref.shape[0]
     table[:half, :] = table_ref[...].astype(F32)
     table[half:, :] = other_ref[...].astype(F32)
+    size = parts[0].shape[0]
+    for d in range(members):
+        states[d * size : (d + 1) * size, :] = parts[d][...].astype(F32)
+    states[members * size :, :] = jnp.zeros((states.shape[0] - members * size, LANE), F32)
     for m in range(members):
         slopes[m * rows + rows - 8 : (m + 1) * rows, :] = jnp.zeros((8, LANE), F32)
     def fetch(j, turn):
@@ -253,7 +265,7 @@
             count = min(8, PART - low)
             start = turn * LANE + low
             f = [
-                held[start + m * PAD : start + m * PAD + 8, :] + parts_ref[m, :, here][low : low + 8].astype(F32)
+                held[pl.ds(pl.multiple_of(start + names[m] * PAD, 8), 8), :] + states[pl.ds(m * size + low * blocks + j, 8, stride=blocks), :]
                 for m in range(members)
             ]
             obs = seen[low : low + 8, here]
@@ -275,7 +287,7 @@
                 r = lax.rsqrt(q)
                 near = q * r if near is None else near + q * r
                 value = area * (miss * r - slope[m] * (1.0 / (members - 1)))
-                slopes[pl.ds(m * rows + low * blocks + j, count, stride=blocks), :] = value[:count]
+                slopes[pl.ds(names[m] * rows + low * blocks + j, count, stride=blocks), :] = value[:count]
             pairs = (2.0 * pairs + 0.1 * members) * (1.0 / (2.0 * members * (members - 1)))
             value = area * (near * (1.0 / members) - pairs)
             slopes[pl.ds(spare + low * per_member, count, stride=per_member), :] = value[:count]
@@ -333,15 +345,17 @@
     shape = jax.ShapeDtypeStruct
     place = lax.axis_index("space")
     core = place % 2
-    slots, ids, parts = pl.pallas_call(
+    member = lax.axis_index("ens")
+    held = -(-PART * blocks // 16) * 16
+    slots, ids, *parts = pl.pallas_call(
         pack_kernel,
         out_shape=(
             shape((spaces * SENT, LANE), BF16),
             shape((blocks, LANE), jnp.int32),
-            shape((members, PAD, points), BF16),
+            *[shape((held, LANE), BF16)] * members,
         ),
         in_specs=[SM] + [HBM] * 3,
-        out_specs=(VM,) * 3,
+        out_specs=(VM,) * (2 + members),
         scratch_shapes=[
             pltpu.VMEM((variables, points), BF16),
             pltpu.VMEM((blocks, LANE), jnp.int32),
@@ -349,6 +363,7 @@
             pltpu.VMEM((LANE, points), F32),
             pltpu.VMEM((points, LANE), F32),
             pltpu.VMEM((spaces * SLOTS, LANE), F32),
+            pltpu.VMEM(((members - 1) * PART * blocks + held, LANE), F32),
             pltpu.VMEM((blocks, LANE), jnp.int32),
             pltpu.SMEM((blocks, LANE), jnp.int32),
             pltpu.SemaphoreType.DMA((4,)),
@@ -357,14 +372,18 @@
         cost_estimate=cost(1.5e8, 8e6),
         name="pack",
     )(
-        core.astype(jnp.int32).reshape(1),
+        jnp.stack([core, member]).astype(jnp.int32),
         stay(initial_states[0]),
         stay(owner.reshape(blocks, LANE)),
         stay(node_local.reshape(blocks, LANE)),
     )
     got = lax.all_to_all(slots.reshape(spaces, SENT, LANE), "space", split_axis=0, concat_axis=0, tiled=True)
-    got, parts = lax.optimization_barrier((got, parts))
-    parts = lax.all_to_all(parts, "ens", split_axis=0, concat_axis=0, tiled=True)
+    for d in (3, 5, 2, 6, 1, 7, 4):
+        parts[d] = lax.ppermute(parts[d], "ens", [(i, (i + d) % members) for i in range(members)])
+    soon = (3, 5, 2, 6, 1, 7)
+    got, *moved = lax.optimization_barrier((got, *[parts[d] for d in soon]))
+    for d, part in zip(soon, moved):
+        parts[d] = part
     normed, source = pl.pallas_call(
         encode_kernel,
         out_shape=(shape((nodes, width), BF16), shape((nodes, width), BF16)),
@@ -385,6 +404,7 @@
         norm_factor.reshape(1, width),
         stay(sender_matrix),
     )
+    source, parts[4] = lax.optimization_barrier((source, parts[4]))
     sibling = lax.ppermute(source, "space", [(i, i ^ 1) for i in range(spaces)])
     other = lax.ppermute(source, "space", [(i, (i + 2 * (i % 2) - 1) % spaces) for i in range(spaces)])
     home = adjacent_vertex_ids // nodes
@@ -405,7 +425,7 @@
         cost_estimate=cost(2e9, 4e6),
         name="near",
     )(
-        lax.axis_index("ens").astype(jnp.int32).reshape(1),
+        member.astype(jnp.int32).reshape(1),
         near,
         normed,
         sibling,
@@ -429,7 +449,7 @@
         cost_estimate=cost(6e9, 4e6, 4.2e6),
         name="process",
     )(near, half, normed, other, stay(link_update_matrix), mesh_to_grid_matrix.T)
-    decoded, parts = lax.optimization_barrier((decoded, parts))
+    decoded, *parts[1:] = lax.optimization_barrier((decoded, *parts[1:]))
     decoded = lax.all_to_all(decoded, "ens", split_axis=0, concat_axis=0, tiled=True)
     decoded = decoded.reshape(members * PAD, nodes).T
     table = lax.all_to_all(
@@ -445,10 +465,11 @@
     slopes = pl.pallas_call(
         crps_kernel,
         out_shape=shape((members, rows, LANE), BF16),
-        in_specs=[SM] + [VM] * 5,
+        in_specs=[SM] * 2 + [VM] * (4 + members),
         out_specs=VM,
         scratch_shapes=[
             pltpu.VMEM((spaces * nodes, LANE), F32),
+            pltpu.VMEM((members * held + (PAD - PART) * blocks, LANE), F32),
             pltpu.VMEM((members * rows, LANE), F32),
             pltpu.VMEM((2 * LANE, LANE), F32),
             pltpu.VMEM((2 * members * PAD, LANE), F32),
@@ -457,12 +478,13 @@
         cost_estimate=cost(5e9, 6e6, 2e6),
         name="crps",
     )(
+        member.astype(jnp.int32).reshape(1),
         ids,
         table,
         table_other,
-        parts,
         seen,
         area.reshape(blocks, LANE),
+        *parts,
     )
     slopes = lax.all_to_all(slopes, "ens", split_axis=0, concat_axis=0, tiled=True)
     crps, grads = pl.pallas_call(

time: 131 us -> 126 us (0.962)
  blocking collectives: 79.8 us -> 56.4 us
  starting transfers between devices: 12.5 us -> 30.2 us
    all_to_all x1 -> x0, blocking collectives: 28.7 us -> none  [local(): lax.all_to_all(slots.reshape(spaces, SENT, LANE), 'space', split_axis=0,...]
    ppermute x0 -> x7, starting transfers between devices: none -> 17.7 us  [local(): lax.ppermute(parts[d], 'ens', [(i, (i + d) % members) for i in range(memb...]
    all_to_all x1, blocking collectives: 12 us -> 14.9 us  [local(): lax.all_to_all(decoded, 'ens', split_axis=0, concat_axis=0, tiled=True)]
    all_to_all x1, blocking collectives: 14.5 us -> 16.9 us  [local(): lax.all_to_all(jnp.broadcast_to(decoded[None], (spaces // 2, nodes, membe...]
    ppermute x1, starting transfers between devices: 3.56 us -> 2.07 us  [local(): lax.ppermute(table, 'space', [(i, i ^ 1) for i in range(spaces)])]
  transfers between devices with their start and end apart: 4 -> 11, of which waited for: 4 -> 4; matrix products, arithmetic and copies ran while one was open for 0% -> 0% of each run, Pallas kernels for 14% -> 10%
where the time goes in v2:
time: 126 us; the launch traced here: 125 us
  blocking collectives  56.4 us (45%)
  Pallas kernels  32.8 us (26%)
  starting transfers between devices  30.2 us (24%)
  waiting for transfers between devices  4.87 us (4%)
    all_to_all x1, blocking collectives, local(): lax.all_to_all(slopes, 'ens', split_axis=0, concat_axis=0, tiled=True)  24.6 us
    ppermute x7, starting transfers between devices, local(): lax.ppermute(parts[d], 'ens', [(i, (i + d) % members) for i in range(memb...  17.7 us
    all_to_all x1, blocking collectives, local(): lax.all_to_all(jnp.broadcast_to(decoded[None], (spaces // 2, nodes, membe...  16.9 us
    all_to_all x1, blocking collectives, local(): lax.all_to_all(decoded, 'ens', split_axis=0, concat_axis=0, tiled=True)  14.9 us
    all_to_all x1, starting transfers between devices, local(): lax.all_to_all(slots.reshape(spaces, SENT, LANE), 'space', split_axis=0,...  8.6 us
    pallas_call x1, Pallas kernels, local(): pl.pallas_call(encode_kernel, out_shape=(shape((nodes, width), BF16), sha...  8.42 us
    pallas_call x1, Pallas kernels, local(): pl.pallas_call(process_kernel, out_shape=shape((members, PAD, nodes), BF1...  6.74 us
    pallas_call x1, Pallas kernels, local(): pl.pallas_call(pack_kernel, out_shape=(shape((spaces * SENT, LANE), BF16)...  6.5 us
  transfers between devices with their start and end apart: 11, of which 4 were waited for; matrix products, arithmetic and copies ran while one was open for 0% of the time, Pallas kernels for 10%

profile of v2, /device:TPU:1, one launch (start us, length us, event | category | flops | bytes accessed | tf_op | source)
XLA Modules:
  0.0 125.5 jit_solution(14773033929126075183)
XLA Ops:
  0.6 0.0 copy-start.4
  0.6 0.0 copy-start
  0.7 0.0 copy-start.1
  0.7 0.1 pad_add_fusion.core_ref
  0.7 6.5 %pack.1 = (bf16[5120,128]{1,0:T(8,128)(2,1)}, s32[24,128]{1,0:T(8,128)S(1)}, bf16[320,128]{1,0:T(8,128)(2,1)S(1)}, bf16[320,128]{1,0:T(8,128)(2,1)S(1)}, bf16[32...) custom-call(s32[2]{0:T(128)S(1)} %pad_add_fusion.core_ref, ...), custom_call_target="tpu_custom_call" | custom-call | flops 150000000 | bytes 8000000 | tf_op jit(solution)/shard_map/pack/pallas_call | solution.py:350
  7.3 8.6 %all-to-all-start = ((bf16[32,160,128]{2,1,0:T(8,128)(2,1)}), bf16[32,160,128]{2,1,0:T(8,128)(2,1)S(1)}, u32[]{:S(2)}, u32[]{:S(2)}) async-start(bf16[32,160,128]{2,1,0:T(8,128)(2,1)} %bitcast.5), calls=%async_computation | async-start | bytes 2621440 | tf_op jit(solution)/shard_map/all_to_all | solution.py:380
  15.9 4.4 %collective-permute-start = (bf16[320,128]{1,0:T(8,128)(2,1)S(1)}, bf16[320,128]{1,0:T(8,128)(2,1)S(1)}, u32[]{:S(2)}, u32[]{:S(2)}) collective-permute-start(bf16[320,128]{1,0:T(8,128)(2,1)S(1)} %get-tuple-element.37), channel_id=1, source_target_pairs={{0,96},{32,128},{64,160},{96,192},{128,224},{160,0},{192,32},{224,... | collective-permute-start | bytes 245768 | tf_op jit(solution)/shard_map/ppermute | solution.py:382
  20.3 2.2 %collective-permute-start.1 = (bf16[320,128]{1,0:T(8,128)(2,1)S(1)}, bf16[320,128]{1,0:T(8,128)(2,1)S(1)}, u32[]{:S(2)}, u32[]{:S(2)}) collective-permute-start(bf16[320,128]{1,0:T(8,128)(2,1)S(1)} %get-tuple-element.38), channel_id=1, source_target_pairs={{0,160},{32,192},{64,224},{96,0},{128,32},{160,64},{192,96},{224,1... | collective-permute-start | bytes 245768 | tf_op jit(solution)/shard_map/ppermute | solution.py:382
  22.5 1.2 collective-permute-start.2
  23.7 2.7 %collective-permute-start.3 = (bf16[320,128]{1,0:T(8,128)(2,1)S(1)}, bf16[320,128]{1,0:T(8,128)(2,1)S(1)}, u32[]{:S(2)}, u32[]{:S(2)}) collective-permute-start(bf16[320,128]{1,0:T(8,128)(2,1)S(1)} %get-tuple-element.40), channel_id=1, source_target_pairs={{0,192},{32,224},{64,0},{96,32},{128,64},{160,96},{192,128},{224,1... | collective-permute-start | bytes 245768 | tf_op jit(solution)/shard_map/ppermute | solution.py:382
  26.4 0.4 collective-permute-start.4
  26.8 0.0 collective-permute-done.rest_3_
  26.8 2.3 %collective-permute-start.5 = (bf16[320,128]{1,0:T(8,128)(2,1)S(1)}, bf16[320,128]{1,0:T(8,128)(2,1)S(1)}, u32[]{:S(2)}, u32[]{:S(2)}) collective-permute-start(bf16[320,128]{1,0:T(8,128)(2,1)S(1)} %get-tuple-element.42), channel_id=1, source_target_pairs={{0,224},{32,0},{64,32},{96,64},{128,96},{160,128},{192,160},{224,1... | collective-permute-start | bytes 245768 | tf_op jit(solution)/shard_map/ppermute | solution.py:382
  29.1 0.0 collective-permute-done.1.rest_5_
  29.1 4.5 %collective-permute-start.6 = (bf16[320,128]{1,0:T(8,128)(2,1)S(1)}, bf16[320,128]{1,0:T(8,128)(2,1)S(1)}, u32[]{:S(2)}, u32[]{:S(2)}) collective-permute-start(bf16[320,128]{1,0:T(8,128)(2,1)S(1)} %get-tuple-element.46), channel_id=1, source_target_pairs={{0,128},{32,160},{64,192},{96,224},{128,0},{160,32},{192,64},{224,... | collective-permute-start | bytes 245768 | tf_op jit(solution)/shard_map/ppermute | solution.py:382
  33.6 0.0 collective-permute-done.2.rest_2_
  33.6 0.0 collective-permute-done.3.rest_6_
  33.6 0.0 collective-permute-done.4.rest_1_
  33.6 0.9 collective-permute-done.5.rest_7_
  34.5 1.1 all-to-all-done
  35.7 0.0 copy-done.4
  35.7 0.0 copy-done
  35.7 0.0 copy-done.1
  35.7 0.0 copy-start.5
  35.7 8.4 %encode.1 = (bf16[128,1024]{1,0:T(8,128)(2,1)S(1)}, bf16[128,1024]{1,0:T(8,128)(2,1)S(1)}) custom-call(bf16[5120,128]{1,0:T(8,128)(2,1)S(1)} %bitcast.15, bf16[100,1024]{1,0:T(8,128)(2,1)S(1)} %copy-done.1, bf16[128,1024]{1,0:T(8,128)(2,1)S(1)} %copy-done, f32[1,1024]{1,0:T(1,128)S(1)} %bitcast.20, bf16[1024,1024]{1,0:T(8,128)(2,1)} %sender_ref.1), custom_call_target="tpu_custom_call" | custom-call | flops 4000000000 | bytes 8000000 | tf_op jit(solution)/shard_map/encode/pallas_call | solution.py:387
  44.1 0.0 collective-permute-done.6.rest_4_
  44.1 0.5 collective-permute-start.7
  44.6 0.0 copy-done.5
  44.6 0.1 copy.21
  44.7 1.3 %collective-permute-start.8 = (bf16[128,1024]{1,0:T(8,128)(2,1)S(1)}, bf16[128,1024]{1,0:T(8,128)(2,1)S(1)}, u32[]{:S(2)}, u32[]{:S(2)}) collective-permute-start(bf16[128,1024]{1,0:T(8,128)(2,1)S(1)} %get-tuple-element.47.own_ref), channel_id=1, source_target_pairs={{0,31},{1,2},{2,1},{3,4},{4,3},{5,6},{6,5},{7,8},{8,7},{9,10},{10,... | collective-permute-start | bytes 786440 | tf_op jit(solution)/shard_map/ppermute | solution.py:409
  46.0 0.1 fusion.near_ref
  46.1 0.0 collective-permute-done.7.sibling_ref
  46.1 0.0 copy-start.2
  46.1 3.5 %near.1 = (f32[2048,1024]{1,0:T(8,128)S(1)}, f32[16,3072]{1,0:T(8,128)S(1)}) custom-call(s32[1]{0:T(128)} %bitcast.member_ref, s32[128,16]{1,0:T(8,128)S(1)} %fusion.near_ref, bf16[128,1024]{1,0:T(8,128)(2,1)S(1)} %get-tuple-element.44.normed_ref, bf16[128,1024]{1,0:T(8,128)(2,1)S(1)} %collective-permute-done.7.sibling_ref, ...), custom_call_target="tpu_custom_call" | custom-call | flops 2000000000 | bytes 4000000 | tf_op jit(solution)/shard_map/near/pallas_call | solution.py:413
  49.6 1.3 collective-permute-done.8.other_ref
  50.9 0.0 copy-done.2
  50.9 0.0 copy-start.3
  50.9 6.7 %process.1 = bf16[8,16,128]{2,1,0:T(8,128)(2,1)S(1)} custom-call(s32[128,16]{1,0:T(8,128)S(1)} %fusion.near_ref, f32[2048,1024]{1,0:T(8,128)S(1)} %get-tuple-element.48.half_ref, bf16[128,1024]{1,0:T(8,128)(2,1)S(1)} %get-tuple-element.44.normed_ref, bf16[128,1024]{1,0:T(8,128)(2,1)S(1)} %collective-permute-done.8.other_ref, bf16[1024,1024]{1,0:T(8,128)(2,1)} %link_ref.1, ...), custom_call_target="tpu_custom_call" | custom-call | flops 6000000000 | bytes 4000000 | tf_op jit(solution)/shard_map/process/pallas_call | solution.py:436
  57.6 14.9 %all_to_all.20 = bf16[8,16,128]{2,1,0:T(8,128)(2,1)S(1)} all-to-all(bf16[8,16,128]{2,1,0:T(8,128)(2,1)S(1)} %process.1), channel_id=1, replica_groups=mesh['ens'=8,'space'=32] {'ens'}, dimensions={0} | all-to-all | bytes 65536 | tf_op jit(solution)/shard_map/all_to_all | solution.py:453
  72.5 0.1 copy.25
  72.6 0.1 broadcast_in_dim.15
  72.7 16.9 %all_to_all.21 = bf16[16,128,128]{2,1,0:T(8,128)(2,1)S(1)} all-to-all(bf16[16,128,128]{2,1,0:T(8,128)(2,1)S(1)} %broadcast_in_dim.15), channel_id=1, replica_groups={{0,2,4,6,8,10,12,14,16,18,20,22,24,26,28,30},{1,3,5,7,9,11,13,15,17,19,..., dimensions={0} | all-to-all | bytes 1048576 | tf_op jit(solution)/shard_map/all_to_all | solution.py:455
  89.7 2.1 %collective-permute-start.9 = (bf16[2048,128]{1,0:T(8,128)(2,1)S(1)}, bf16[2048,128]{1,0:T(8,128)(2,1)S(1)}, u32[]{:S(2)}, u32[]{:S(2)}) collective-permute-start(bf16[2048,128]{1,0:T(8,128)(2,1)S(1)} %bitcast.16), channel_id=1, source_target_pairs={{0,1},{1,0},{2,3},{3,2},{4,5},{5,4},{6,7},{7,6},{8,9},{9,8},{10,11... | collective-permute-start | bytes 1572872 | tf_op jit(solution)/shard_map/ppermute | solution.py:463
  91.7 1.5 %collective-permute-done.9.other_ref = bf16[2048,128]{1,0:T(8,128)(2,1)S(1)} collective-permute-done((bf16[2048,128]{1,0:T(8,128)(2,1)S(1)}, bf16[2048,128]{1,0:T(8,128)(2,1)S(1)}, u32[]{:S(2)}, u32[]{:S(2)}) %collective-permute-start.9) | collective-permute-done | bytes 524320 | tf_op jit(solution)/shard_map/ppermute | solution.py:463
  93.3 0.0 copy-done.3
  93.3 6.4 %crps.1 = bf16[8,352,128]{2,1,0:T(8,128)(2,1)S(1)} custom-call(s32[1]{0:T(128)} %bitcast.member_ref, s32[24,128]{1,0:T(8,128)S(1)} %get-tuple-element.35.ids_ref, bf16[2048,128]{1,0:T(8,128)(2,1)S(1)} %bitcast.17, bf16[2048,128]{1,0:T(8,128)(2,1)S(1)} %collective-permute-done.9.other_ref, f32[16,3072]{1,0:T(8,128)S(1)} %get-tuple-element.57.seen, ...), custom_call_target="tpu_custom_call" | custom-call | flops 5000000000 | bytes 6000000 | tf_op jit(solution)/shard_map/crps/pallas_call | solution.py:465
  99.7 24.6 %all_to_all.22.got_ref = bf16[8,352,128]{2,1,0:T(8,128)(2,1)S(1)} all-to-all(bf16[8,352,128]{2,1,0:T(8,128)(2,1)S(1)} %crps.1), channel_id=1, replica_groups=mesh['ens'=8,'space'=32] {'ens'}, dimensions={0} | all-to-all | bytes 1441792 | tf_op jit(solution)/shard_map/all_to_all | solution.py:489
  124.3 1.2 unpack.1
Async XLA Ops:
  0.6 35.0 %copy-start.4 = (f32[1024]{0:T(1024)S(1)}, f32[1024]{0:T(1024)}, u32[]{:S(2)}) copy-start(f32[1024]{0:T(1024)} %param.18) | copy-start | bytes 12292
  0.6 35.0 %copy-start = (bf16[128,1024]{1,0:T(8,128)(2,1)S(1)}, bf16[128,1024]{1,0:T(8,128)(2,1)}, u32[]{:S(2)}) copy-start(bf16[128,1024]{1,0:T(8,128)(2,1)} %latent_ref.1) | copy-start | bytes 786436
  0.7 35.0 %copy-start.1 = (bf16[100,1024]{1,0:T(8,128)(2,1)S(1)}, bf16[100,1024]{1,0:T(8,128)(2,1)}, u32[]{:S(2)}) copy-start(bf16[100,1024]{1,0:T(8,128)(2,1)} %embed_ref.1) | copy-start | bytes 614404
  7.3 28.4 %all-to-all-start = ((bf16[32,160,128]{2,1,0:T(8,128)(2,1)}), bf16[32,160,128]{2,1,0:T(8,128)(2,1)S(1)}, u32[]{:S(2)}, u32[]{:S(2)}) async-start(bf16[32,160,128]{2,1,0:T(8,128)(2,1)} %bitcast.5), calls=%async_computation | async-start | bytes 2621440 | tf_op jit(solution)/shard_map/all_to_all | solution.py:380
  15.9 11.0 %collective-permute-start = (bf16[320,128]{1,0:T(8,128)(2,1)S(1)}, bf16[320,128]{1,0:T(8,128)(2,1)S(1)}, u32[]{:S(2)}, u32[]{:S(2)}) collective-permute-start(bf16[320,128]{1,0:T(8,128)(2,1)S(1)} %get-tuple-element.37), channel_id=1, source_target_pairs={{0,96},{32,128},{64,160},{96,192},{128,224},{160,0},{192,32},{224,... | collective-permute-start | bytes 245768 | tf_op jit(solution)/shard_map/ppermute | solution.py:382
  20.3 8.8 %collective-permute-start.1 = (bf16[320,128]{1,0:T(8,128)(2,1)S(1)}, bf16[320,128]{1,0:T(8,128)(2,1)S(1)}, u32[]{:S(2)}, u32[]{:S(2)}) collective-permute-start(bf16[320,128]{1,0:T(8,128)(2,1)S(1)} %get-tuple-element.38), channel_id=1, source_target_pairs={{0,160},{32,192},{64,224},{96,0},{128,32},{160,64},{192,96},{224,1... | collective-permute-start | bytes 245768 | tf_op jit(solution)/shard_map/ppermute | solution.py:382
  22.5 11.1 %collective-permute-start.2 = (bf16[320,128]{1,0:T(8,128)(2,1)S(1)}, bf16[320,128]{1,0:T(8,128)(2,1)S(1)}, u32[]{:S(2)}, u32[]{:S(2)}) collective-permute-start(bf16[320,128]{1,0:T(8,128)(2,1)S(1)} %get-tuple-element.39), channel_id=1, source_target_pairs={{0,64},{32,96},{64,128},{96,160},{128,192},{160,224},{192,0},{224,... | collective-permute-start | bytes 245768 | tf_op jit(solution)/shard_map/ppermute | solution.py:382
  23.7 9.9 %collective-permute-start.3 = (bf16[320,128]{1,0:T(8,128)(2,1)S(1)}, bf16[320,128]{1,0:T(8,128)(2,1)S(1)}, u32[]{:S(2)}, u32[]{:S(2)}) collective-permute-start(bf16[320,128]{1,0:T(8,128)(2,1)S(1)} %get-tuple-element.40), channel_id=1, source_target_pairs={{0,192},{32,224},{64,0},{96,32},{128,64},{160,96},{192,128},{224,1... | collective-permute-start | bytes 245768 | tf_op jit(solution)/shard_map/ppermute | solution.py:382
  26.4 7.2 %collective-permute-start.4 = (bf16[320,128]{1,0:T(8,128)(2,1)S(1)}, bf16[320,128]{1,0:T(8,128)(2,1)S(1)}, u32[]{:S(2)}, u32[]{:S(2)}) collective-permute-start(bf16[320,128]{1,0:T(8,128)(2,1)S(1)} %get-tuple-element.41), channel_id=1, source_target_pairs={{0,32},{32,64},{64,96},{96,128},{128,160},{160,192},{192,224},{224... | collective-permute-start | bytes 245768 | tf_op jit(solution)/shard_map/ppermute | solution.py:382
  26.8 7.7 %collective-permute-start.5 = (bf16[320,128]{1,0:T(8,128)(2,1)S(1)}, bf16[320,128]{1,0:T(8,128)(2,1)S(1)}, u32[]{:S(2)}, u32[]{:S(2)}) collective-permute-start(bf16[320,128]{1,0:T(8,128)(2,1)S(1)} %get-tuple-element.42), channel_id=1, source_target_pairs={{0,224},{32,0},{64,32},{96,64},{128,96},{160,128},{192,160},{224,1... | collective-permute-start | bytes 245768 | tf_op jit(solution)/shard_map/ppermute | solution.py:382
  29.1 15.0 %collective-permute-start.6 = (bf16[320,128]{1,0:T(8,128)(2,1)S(1)}, bf16[320,128]{1,0:T(8,128)(2,1)S(1)}, u32[]{:S(2)}, u32[]{:S(2)}) collective-permute-start(bf16[320,128]{1,0:T(8,128)(2,1)S(1)} %get-tuple-element.46), channel_id=1, source_target_pairs={{0,128},{32,160},{64,192},{96,224},{128,0},{160,32},{192,64},{224,... | collective-permute-start | bytes 245768 | tf_op jit(solution)/shard_map/ppermute | solution.py:382
  35.7 8.9 %copy-start.5 = (s32[128,16]{0,1:T(8,128)S(1)}, s32[128,16]{0,1:T(8,128)}, u32[]{:S(2)}) copy-start(s32[128,16]{0,1:T(8,128)} %param.16) | copy-start | bytes 24580
  44.1 1.9 %collective-permute-start.7 = (bf16[128,1024]{1,0:T(8,128)(2,1)S(1)}, bf16[128,1024]{1,0:T(8,128)(2,1)S(1)}, u32[]{:S(2)}, u32[]{:S(2)}) collective-permute-start(bf16[128,1024]{1,0:T(8,128)(2,1)S(1)} %get-tuple-element.47.own_ref), channel_id=1, source_target_pairs={{0,1},{1,0},{2,3},{3,2},{4,5},{5,4},{6,7},{7,6},{8,9},{9,8},{10,11... | collective-permute-start | bytes 786440 | tf_op jit(solution)/shard_map/ppermute | solution.py:408
  44.7 6.2 %collective-permute-start.8 = (bf16[128,1024]{1,0:T(8,128)(2,1)S(1)}, bf16[128,1024]{1,0:T(8,128)(2,1)S(1)}, u32[]{:S(2)}, u32[]{:S(2)}) collective-permute-start(bf16[128,1024]{1,0:T(8,128)(2,1)S(1)} %get-tuple-element.47.own_ref), channel_id=1, source_target_pairs={{0,31},{1,2},{2,1},{3,4},{4,3},{5,6},{6,5},{7,8},{8,7},{9,10},{10,... | collective-permute-start | bytes 786440 | tf_op jit(solution)/shard_map/ppermute | solution.py:409
  46.1 4.8 %copy-start.2 = (bf16[1024,100]{0,1:T(8,128)(2,1)S(1)}, bf16[1024,100]{0,1:T(8,128)(2,1)}, u32[]{:S(2)}) copy-start(bf16[1024,100]{0,1:T(8,128)(2,1)} %param.23) | copy-start | bytes 614404
  50.9 42.4 %copy-start.3 = (f32[3072]{0:T(1024)S(1)}, f32[3072]{0:T(1024)}, u32[]{:S(2)}) copy-start(f32[3072]{0:T(1024)} %param.25) | copy-start | bytes 36868
  89.7 3.6 %collective-permute-start.9 = (bf16[2048,128]{1,0:T(8,128)(2,1)S(1)}, bf16[2048,128]{1,0:T(8,128)(2,1)S(1)}, u32[]{:S(2)}, u32[]{:S(2)}) collective-permute-start(bf16[2048,128]{1,0:T(8,128)(2,1)S(1)} %bitcast.16), channel_id=1, source_target_pairs={{0,1},{1,0},{2,3},{3,2},{4,5},{5,4},{6,7},{7,6},{8,9},{9,8},{10,11... | collective-permute-start | bytes 1572872 | tf_op jit(solution)/shard_map/ppermute | solution.py:463

commit v3 on v2

--- a/solution.py
+++ b/solution.py
@@ -163,8 +163,10 @@
     own_ref,
     receiver_hbm,
     observed_hbm,
+    link_hbm,
     half_ref,
     seen_ref,
+    link_ref,
     receiver,
     observed,
     beside,
@@ -173,6 +175,7 @@
     loads = [
         pltpu.make_async_copy(receiver_hbm, receiver, sems.at[0]),
         pltpu.make_async_copy(observed_hbm, observed, sems.at[1]),
+        pltpu.make_async_copy(link_hbm, link_ref, sems.at[2]),
     ]
     for load in loads:
         load.start()
@@ -199,12 +202,12 @@
             seen_ref[...] = jnp.zeros_like(seen_ref)
             seen_ref[:count, :] = observed[c * PART : c * PART + count, :]
 
+    loads[2].wait()
+
 
 def process_kernel(
-    near_ref, half_ref, normed_ref, other_ref, link_ref, decode_ref, out_ref, edges, total, spaced, link, sem
+    near_ref, half_ref, normed_ref, other_ref, link_ref, decode_ref, out_ref, edges, total, spaced
 ):
-    copy = pltpu.make_async_copy(link_ref, link, sem)
-    copy.start()
     nodes, fanout = near_ref.shape
     variables = decode_ref.shape[0]
     group = 4
@@ -215,9 +218,8 @@
         ).astype(BF16)
         h = half_ref[g * nodes : (g + group) * nodes, :] + jnp.dot(hot, other_ref[...], preferred_element_type=F32)
         edges[g * nodes : (g + group) * nodes, :] = (h + h * jnp.tanh(h)).astype(BF16)
-    copy.wait()
     for g in range(0, fanout, group):
-        z = jnp.dot(edges[g * nodes : (g + group) * nodes, :], link[...], preferred_element_type=F32)
+        z = jnp.dot(edges[g * nodes : (g + group) * nodes, :], link_ref[...], preferred_element_type=F32)
         z = z + z * jnp.tanh(0.5 * z)
         part = sum(z[k * nodes : (k + 1) * nodes] for k in range(group))
         if g == 0:
@@ -380,7 +382,7 @@
     got = lax.all_to_all(slots.reshape(spaces, SENT, LANE), "space", split_axis=0, concat_axis=0, tiled=True)
     for d in (3, 5, 2, 6, 1, 7, 4):
         parts[d] = lax.ppermute(parts[d], "ens", [(i, (i + d) % members) for i in range(members)])
-    soon = (3, 5, 2, 6, 1, 7)
+    soon = (3, 5)
     got, *moved = lax.optimization_barrier((got, *[parts[d] for d in soon]))
     for d, part in zip(soon, moved):
         parts[d] = part
@@ -404,22 +406,24 @@
         norm_factor.reshape(1, width),
         stay(sender_matrix),
     )
-    source, parts[4] = lax.optimization_barrier((source, parts[4]))
+    source, *moved = lax.optimization_barrier((source, *[parts[d] for d in (2, 6, 1, 7, 4)]))
+    for d, part in zip((2, 6, 1, 7, 4), moved):
+        parts[d] = part
     sibling = lax.ppermute(source, "space", [(i, i ^ 1) for i in range(spaces)])
     other = lax.ppermute(source, "space", [(i, (i + 2 * (i % 2) - 1) % spaces) for i in range(spaces)])
     home = adjacent_vertex_ids // nodes
     slab = jnp.where(home == place, 1, jnp.where(home == place + 1 - 2 * core, 0, 2))
     near = slab * nodes + adjacent_vertex_ids % nodes
-    half, seen = pl.pallas_call(
+    half, seen, link = pl.pallas_call(
         near_kernel,
-        out_shape=(shape((fanout * nodes, width), F32), shape((PAD, points), F32)),
-        in_specs=[SM] + [VM] * 4 + [HBM] * 2,
-        out_specs=(VM, VM),
+        out_shape=(shape((fanout * nodes, width), F32), shape((PAD, points), F32), shape((width, width), BF16)),
+        in_specs=[SM] + [VM] * 4 + [HBM] * 3,
+        out_specs=(VM,) * 3,
         scratch_shapes=[
             pltpu.VMEM((width, width), BF16),
             pltpu.VMEM((variables, points), F32),
             pltpu.VMEM((2 * nodes, width), BF16),
-            pltpu.SemaphoreType.DMA((2,)),
+            pltpu.SemaphoreType.DMA((3,)),
         ],
         compiler_params=params(16),
         cost_estimate=cost(2e9, 4e6),
@@ -432,23 +436,22 @@
         source,
         stay(receiver_matrix),
         stay(observed),
+        stay(link_update_matrix),
     )
     decoded = pl.pallas_call(
         process_kernel,
         out_shape=shape((members, PAD, nodes), BF16),
-        in_specs=[VM] * 4 + [HBM, VM],
+        in_specs=[VM] * 6,
         out_specs=VM,
         scratch_shapes=[
             pltpu.VMEM((fanout * nodes, width), BF16),
             pltpu.VMEM((nodes, width), F32),
             pltpu.VMEM((members * PAD, nodes), F32),
-            pltpu.VMEM((width, width), BF16),
-            pltpu.SemaphoreType.DMA,
         ],
         compiler_params=params(20),
         cost_estimate=cost(6e9, 4e6, 4.2e6),
         name="process",
-    )(near, half, normed, other, stay(link_update_matrix), mesh_to_grid_matrix.T)
+    )(near, half, normed, other, link, mesh_to_grid_matrix.T)
     decoded, *parts[1:] = lax.optimization_barrier((decoded, *parts[1:]))
     decoded = lax.all_to_all(decoded, "ens", split_axis=0, concat_axis=0, tiled=True)
     decoded = decoded.reshape(members * PAD, nodes).T

time: 126 us -> 124 us (0.984)
  blocking collectives: 56.4 us -> 54.2 us
  starting transfers between devices: 30.2 us -> 31.5 us
    all_to_all x1, blocking collectives: 16.9 us -> 14.8 us  [local(): lax.all_to_all(jnp.broadcast_to(decoded[None], (spaces // 2, nodes, membe...]
    ppermute x1, starting transfers between devices: 2.07 us -> 3.48 us  [local(): lax.ppermute(table, 'space', [(i, i ^ 1) for i in range(spaces)])]
  transfers between devices with their start and end apart: 11 -> 11, of which waited for: 4 -> 3; matrix products, arithmetic and copies ran while one was open for 0% -> 0% of each run, Pallas kernels for 10% -> 10%
where the time goes in v3:
time: 124 us
  blocking collectives  54.2 us (44%)
  Pallas kernels  32.1 us (26%)
  starting transfers between devices  31.5 us (25%)
  waiting for transfers between devices  4.93 us (4%)
    all_to_all x1, blocking collectives, local(): lax.all_to_all(slopes, 'ens', split_axis=0, concat_axis=0, tiled=True)  24.6 us
    ppermute x7, starting transfers between devices, local(): lax.ppermute(parts[d], 'ens', [(i, (i + d) % members) for i in range(memb...  17.7 us
    all_to_all x1, blocking collectives, local(): lax.all_to_all(decoded, 'ens', split_axis=0, concat_axis=0, tiled=True)  14.9 us
    all_to_all x1, blocking collectives, local(): lax.all_to_all(jnp.broadcast_to(decoded[None], (spaces // 2, nodes, membe...  14.8 us
    all_to_all x1, starting transfers between devices, local(): lax.all_to_all(slots.reshape(spaces, SENT, LANE), 'space', split_axis=0,...  8.6 us
    pallas_call x1, Pallas kernels, local(): pl.pallas_call(encode_kernel, out_shape=(shape((nodes, width), BF16), sha...  8.42 us
    pallas_call x1, Pallas kernels, local(): pl.pallas_call(pack_kernel, out_shape=(shape((spaces * SENT, LANE), BF16)...  6.5 us
    pallas_call x1, Pallas kernels, local(): pl.pallas_call(crps_kernel, out_shape=shape((members, rows, LANE), BF16),...  6.44 us
  transfers between devices with their start and end apart: 11, of which 3 were waited for; matrix products, arithmetic and copies ran while one was open for 0% of the time, Pallas kernels for 10%

profile of v3, /device:TPU:1, one launch (start us, length us, event | category | flops | bytes accessed | tf_op | source)
XLA Modules:
  0.0 124.0 jit_solution(15389583023374992638)
XLA Ops:
  0.6 0.0 copy-start.4
  0.6 0.0 copy-start
  0.7 0.0 copy-start.1
  0.7 0.1 pad_add_fusion.core_ref
  0.7 6.5 %pack.1 = (bf16[5120,128]{1,0:T(8,128)(2,1)}, s32[24,128]{1,0:T(8,128)S(1)}, bf16[320,128]{1,0:T(8,128)(2,1)S(1)}, bf16[320,128]{1,0:T(8,128)(2,1)S(1)}, bf16[32...) custom-call(s32[2]{0:T(128)S(1)} %pad_add_fusion.core_ref, ...), custom_call_target="tpu_custom_call" | custom-call | flops 150000000 | bytes 8000000 | tf_op jit(solution)/shard_map/pack/pallas_call | solution.py:352
  7.3 8.6 %all-to-all-start = ((bf16[32,160,128]{2,1,0:T(8,128)(2,1)}), bf16[32,160,128]{2,1,0:T(8,128)(2,1)S(1)}, u32[]{:S(2)}, u32[]{:S(2)}) async-start(bf16[32,160,128]{2,1,0:T(8,128)(2,1)} %bitcast.5), calls=%async_computation | async-start | bytes 2621440 | tf_op jit(solution)/shard_map/all_to_all | solution.py:382
  15.9 4.4 %collective-permute-start = (bf16[320,128]{1,0:T(8,128)(2,1)S(1)}, bf16[320,128]{1,0:T(8,128)(2,1)S(1)}, u32[]{:S(2)}, u32[]{:S(2)}) collective-permute-start(bf16[320,128]{1,0:T(8,128)(2,1)S(1)} %get-tuple-element.38), channel_id=1, source_target_pairs={{0,96},{32,128},{64,160},{96,192},{128,224},{160,0},{192,32},{224,... | collective-permute-start | bytes 245768 | tf_op jit(solution)/shard_map/ppermute | solution.py:384
  20.3 2.2 %collective-permute-start.1 = (bf16[320,128]{1,0:T(8,128)(2,1)S(1)}, bf16[320,128]{1,0:T(8,128)(2,1)S(1)}, u32[]{:S(2)}, u32[]{:S(2)}) collective-permute-start(bf16[320,128]{1,0:T(8,128)(2,1)S(1)} %get-tuple-element.39), channel_id=1, source_target_pairs={{0,160},{32,192},{64,224},{96,0},{128,32},{160,64},{192,96},{224,1... | collective-permute-start | bytes 245768 | tf_op jit(solution)/shard_map/ppermute | solution.py:384
  22.5 1.2 collective-permute-start.2
  23.7 2.7 %collective-permute-start.3 = (bf16[320,128]{1,0:T(8,128)(2,1)S(1)}, bf16[320,128]{1,0:T(8,128)(2,1)S(1)}, u32[]{:S(2)}, u32[]{:S(2)}) collective-permute-start(bf16[320,128]{1,0:T(8,128)(2,1)S(1)} %get-tuple-element.44), channel_id=1, source_target_pairs={{0,192},{32,224},{64,0},{96,32},{128,64},{160,96},{192,128},{224,1... | collective-permute-start | bytes 245768 | tf_op jit(solution)/shard_map/ppermute | solution.py:384
  26.4 0.4 collective-permute-start.4
  26.8 0.0 collective-permute-done.rest_3_
  26.8 2.3 %collective-permute-start.5 = (bf16[320,128]{1,0:T(8,128)(2,1)S(1)}, bf16[320,128]{1,0:T(8,128)(2,1)S(1)}, u32[]{:S(2)}, u32[]{:S(2)}) collective-permute-start(bf16[320,128]{1,0:T(8,128)(2,1)S(1)} %get-tuple-element.46), channel_id=1, source_target_pairs={{0,224},{32,0},{64,32},{96,64},{128,96},{160,128},{192,160},{224,1... | collective-permute-start | bytes 245768 | tf_op jit(solution)/shard_map/ppermute | solution.py:384
  29.1 0.0 collective-permute-done.1.rest_5_
  29.1 4.5 %collective-permute-start.6 = (bf16[320,128]{1,0:T(8,128)(2,1)S(1)}, bf16[320,128]{1,0:T(8,128)(2,1)S(1)}, u32[]{:S(2)}, u32[]{:S(2)}) collective-permute-start(bf16[320,128]{1,0:T(8,128)(2,1)S(1)} %get-tuple-element.47), channel_id=1, source_target_pairs={{0,128},{32,160},{64,192},{96,224},{128,0},{160,32},{192,64},{224,... | collective-permute-start | bytes 245768 | tf_op jit(solution)/shard_map/ppermute | solution.py:384
  33.6 2.1 %all-to-all-done = bf16[32,160,128]{2,1,0:T(8,128)(2,1)S(1)} async-done(((bf16[32,160,128]{2,1,0:T(8,128)(2,1)}), bf16[32,160,128]{2,1,0:T(8,128)(2,1)S(1)}, u32[]{:S(2)}, u32[]{:S(2)}) %all-to-all-start) | async-done | bytes 1310752 | tf_op jit(solution)/shard_map/all_to_all | solution.py:382
  35.7 0.0 copy-done.4
  35.7 0.0 copy-done
  35.7 0.0 copy-done.1
  35.7 0.0 copy-start.5
  35.7 8.4 %encode.1 = (bf16[128,1024]{1,0:T(8,128)(2,1)S(1)}, bf16[128,1024]{1,0:T(8,128)(2,1)S(1)}) custom-call(bf16[5120,128]{1,0:T(8,128)(2,1)S(1)} %bitcast.15, bf16[100,1024]{1,0:T(8,128)(2,1)S(1)} %copy-done.1, bf16[128,1024]{1,0:T(8,128)(2,1)S(1)} %copy-done, f32[1,1024]{1,0:T(1,128)S(1)} %bitcast.20, bf16[1024,1024]{1,0:T(8,128)(2,1)} %sender_ref.1), custom_call_target="tpu_custom_call" | custom-call | flops 4000000000 | bytes 8000000 | tf_op jit(solution)/shard_map/encode/pallas_call | solution.py:389
  44.1 0.0 collective-permute-done.2.rest_2_
  44.1 0.0 collective-permute-done.3.rest_6_
  44.1 0.0 collective-permute-done.4.rest_1_
  44.1 0.0 collective-permute-done.5.rest_7_
  44.1 0.0 collective-permute-done.6.rest_4_
  44.2 0.5 collective-permute-start.7
  44.6 0.0 copy-done.5
  44.6 0.1 copy.21
  44.7 1.2 collective-permute-start.8
  46.0 0.1 fusion.near_ref
  46.1 0.0 collective-permute-done.7.sibling_ref
  46.1 0.0 copy-start.2
  46.1 3.5 %near.1 = (f32[2048,1024]{1,0:T(8,128)S(1)}, f32[16,3072]{1,0:T(8,128)S(1)}, bf16[1024,1024]{1,0:T(8,128)(2,1)S(1)}) custom-call(s32[1]{0:T(128)} %bitcast.member_ref, s32[128,16]{1,0:T(8,128)S(1)} %fusion.near_ref, bf16[128,1024]{1,0:T(8,128)(2,1)S(1)} %get-tuple-element.41.normed_ref, bf16[128,1024]{1,0:T(8,128)(2,1)S(1)} %collective-permute-done.7.sibling_ref, ...), custom_call_target="tpu_custom_call" | custom-call | flops 2000000000 | bytes 4000000 | tf_op jit(solution)/shard_map/near/pallas_call | solution.py:417
  49.6 1.3 %collective-permute-done.8.other_ref = bf16[128,1024]{1,0:T(8,128)(2,1)S(1)} collective-permute-done((bf16[128,1024]{1,0:T(8,128)(2,1)S(1)}, bf16[128,1024]{1,0:T(8,128)(2,1)S(1)}, u32[]{:S(2)}, u32[]{:S(2)}) %collective-permute-start.8) | collective-permute-done | bytes 262176 | tf_op jit(solution)/shard_map/ppermute | solution.py:413
  50.9 0.0 copy-done.2
  50.9 0.0 copy-start.3
  50.9 6.0 %process.1 = bf16[8,16,128]{2,1,0:T(8,128)(2,1)S(1)} custom-call(s32[128,16]{1,0:T(8,128)S(1)} %fusion.near_ref, f32[2048,1024]{1,0:T(8,128)S(1)} %get-tuple-element.49.half_ref, bf16[128,1024]{1,0:T(8,128)(2,1)S(1)} %get-tuple-element.41.normed_ref, bf16[128,1024]{1,0:T(8,128)(2,1)S(1)} %collective-permute-done.8.other_ref, ...), custom_call_target="tpu_custom_call" | custom-call | flops 6000000000 | bytes 4000000 | tf_op jit(solution)/shard_map/process/pallas_call | solution.py:441
  56.9 14.9 %all_to_all.20 = bf16[8,16,128]{2,1,0:T(8,128)(2,1)S(1)} all-to-all(bf16[8,16,128]{2,1,0:T(8,128)(2,1)S(1)} %process.1), channel_id=1, replica_groups=mesh['ens'=8,'space'=32] {'ens'}, dimensions={0} | all-to-all | bytes 65536 | tf_op jit(solution)/shard_map/all_to_all | solution.py:456
  71.8 0.1 copy.25
  71.9 0.1 broadcast_in_dim.15
  72.0 14.8 %all_to_all.21 = bf16[16,128,128]{2,1,0:T(8,128)(2,1)S(1)} all-to-all(bf16[16,128,128]{2,1,0:T(8,128)(2,1)S(1)} %broadcast_in_dim.15), channel_id=1, replica_groups={{0,2,4,6,8,10,12,14,16,18,20,22,24,26,28,30},{1,3,5,7,9,11,13,15,17,19,..., dimensions={0} | all-to-all | bytes 1048576 | tf_op jit(solution)/shard_map/all_to_all | solution.py:458
  86.8 3.5 %collective-permute-start.9 = (bf16[2048,128]{1,0:T(8,128)(2,1)S(1)}, bf16[2048,128]{1,0:T(8,128)(2,1)S(1)}, u32[]{:S(2)}, u32[]{:S(2)}) collective-permute-start(bf16[2048,128]{1,0:T(8,128)(2,1)S(1)} %bitcast.16), channel_id=1, source_target_pairs={{0,1},{1,0},{2,3},{3,2},{4,5},{5,4},{6,7},{7,6},{8,9},{9,8},{10,11... | collective-permute-start | bytes 1572872 | tf_op jit(solution)/shard_map/ppermute | solution.py:466
  90.3 1.5 %collective-permute-done.9.other_ref = bf16[2048,128]{1,0:T(8,128)(2,1)S(1)} collective-permute-done((bf16[2048,128]{1,0:T(8,128)(2,1)S(1)}, bf16[2048,128]{1,0:T(8,128)(2,1)S(1)}, u32[]{:S(2)}, u32[]{:S(2)}) %collective-permute-start.9) | collective-permute-done | bytes 524320 | tf_op jit(solution)/shard_map/ppermute | solution.py:466
  91.8 0.0 copy-done.3
  91.8 6.4 %crps.1 = bf16[8,352,128]{2,1,0:T(8,128)(2,1)S(1)} custom-call(s32[1]{0:T(128)} %bitcast.member_ref, s32[24,128]{1,0:T(8,128)S(1)} %get-tuple-element.36.ids_ref, bf16[2048,128]{1,0:T(8,128)(2,1)S(1)} %bitcast.17, bf16[2048,128]{1,0:T(8,128)(2,1)S(1)} %collective-permute-done.9.other_ref, f32[16,3072]{1,0:T(8,128)S(1)} %get-tuple-element.59.seen, ...), custom_call_target="tpu_custom_call" | custom-call | flops 5000000000 | bytes 6000000 | tf_op jit(solution)/shard_map/crps/pallas_call | solution.py:468
  98.2 24.6 %all_to_all.22.got_ref = bf16[8,352,128]{2,1,0:T(8,128)(2,1)S(1)} all-to-all(bf16[8,352,128]{2,1,0:T(8,128)(2,1)S(1)} %crps.1), channel_id=1, replica_groups=mesh['ens'=8,'space'=32] {'ens'}, dimensions={0} | all-to-all | bytes 1441792 | tf_op jit(solution)/shard_map/all_to_all | solution.py:492
  122.8 1.2 unpack.1
Async XLA Ops:
  0.6 35.0 %copy-start.4 = (f32[1024]{0:T(1024)S(1)}, f32[1024]{0:T(1024)}, u32[]{:S(2)}) copy-start(f32[1024]{0:T(1024)} %param.18) | copy-start | bytes 12292
  0.6 35.0 %copy-start = (bf16[128,1024]{1,0:T(8,128)(2,1)S(1)}, bf16[128,1024]{1,0:T(8,128)(2,1)}, u32[]{:S(2)}) copy-start(bf16[128,1024]{1,0:T(8,128)(2,1)} %latent_ref.1) | copy-start | bytes 786436
  0.7 35.0 %copy-start.1 = (bf16[100,1024]{1,0:T(8,128)(2,1)S(1)}, bf16[100,1024]{1,0:T(8,128)(2,1)}, u32[]{:S(2)}) copy-start(bf16[100,1024]{1,0:T(8,128)(2,1)} %embed_ref.1) | copy-start | bytes 614404
  7.3 28.4 %all-to-all-start = ((bf16[32,160,128]{2,1,0:T(8,128)(2,1)}), bf16[32,160,128]{2,1,0:T(8,128)(2,1)S(1)}, u32[]{:S(2)}, u32[]{:S(2)}) async-start(bf16[32,160,128]{2,1,0:T(8,128)(2,1)} %bitcast.5), calls=%async_computation | async-start | bytes 2621440 | tf_op jit(solution)/shard_map/all_to_all | solution.py:382
  15.9 11.0 %collective-permute-start = (bf16[320,128]{1,0:T(8,128)(2,1)S(1)}, bf16[320,128]{1,0:T(8,128)(2,1)S(1)}, u32[]{:S(2)}, u32[]{:S(2)}) collective-permute-start(bf16[320,128]{1,0:T(8,128)(2,1)S(1)} %get-tuple-element.38), channel_id=1, source_target_pairs={{0,96},{32,128},{64,160},{96,192},{128,224},{160,0},{192,32},{224,... | collective-permute-start | bytes 245768 | tf_op jit(solution)/shard_map/ppermute | solution.py:384
  20.3 8.8 %collective-permute-start.1 = (bf16[320,128]{1,0:T(8,128)(2,1)S(1)}, bf16[320,128]{1,0:T(8,128)(2,1)S(1)}, u32[]{:S(2)}, u32[]{:S(2)}) collective-permute-start(bf16[320,128]{1,0:T(8,128)(2,1)S(1)} %get-tuple-element.39), channel_id=1, source_target_pairs={{0,160},{32,192},{64,224},{96,0},{128,32},{160,64},{192,96},{224,1... | collective-permute-start | bytes 245768 | tf_op jit(solution)/shard_map/ppermute | solution.py:384
  22.5 21.6 %collective-permute-start.2 = (bf16[320,128]{1,0:T(8,128)(2,1)S(1)}, bf16[320,128]{1,0:T(8,128)(2,1)S(1)}, u32[]{:S(2)}, u32[]{:S(2)}) collective-permute-start(bf16[320,128]{1,0:T(8,128)(2,1)S(1)} %get-tuple-element.43), channel_id=1, source_target_pairs={{0,64},{32,96},{64,128},{96,160},{128,192},{160,224},{192,0},{224,... | collective-permute-start | bytes 245768 | tf_op jit(solution)/shard_map/ppermute | solution.py:384
  23.7 20.4 %collective-permute-start.3 = (bf16[320,128]{1,0:T(8,128)(2,1)S(1)}, bf16[320,128]{1,0:T(8,128)(2,1)S(1)}, u32[]{:S(2)}, u32[]{:S(2)}) collective-permute-start(bf16[320,128]{1,0:T(8,128)(2,1)S(1)} %get-tuple-element.44), channel_id=1, source_target_pairs={{0,192},{32,224},{64,0},{96,32},{128,64},{160,96},{192,128},{224,1... | collective-permute-start | bytes 245768 | tf_op jit(solution)/shard_map/ppermute | solution.py:384
  26.4 17.7 %collective-permute-start.4 = (bf16[320,128]{1,0:T(8,128)(2,1)S(1)}, bf16[320,128]{1,0:T(8,128)(2,1)S(1)}, u32[]{:S(2)}, u32[]{:S(2)}) collective-permute-start(bf16[320,128]{1,0:T(8,128)(2,1)S(1)} %get-tuple-element.45), channel_id=1, source_target_pairs={{0,32},{32,64},{64,96},{96,128},{128,160},{160,192},{192,224},{224... | collective-permute-start | bytes 245768 | tf_op jit(solution)/shard_map/ppermute | solution.py:384
  26.8 17.3 %collective-permute-start.5 = (bf16[320,128]{1,0:T(8,128)(2,1)S(1)}, bf16[320,128]{1,0:T(8,128)(2,1)S(1)}, u32[]{:S(2)}, u32[]{:S(2)}) collective-permute-start(bf16[320,128]{1,0:T(8,128)(2,1)S(1)} %get-tuple-element.46), channel_id=1, source_target_pairs={{0,224},{32,0},{64,32},{96,64},{128,96},{160,128},{192,160},{224,1... | collective-permute-start | bytes 245768 | tf_op jit(solution)/shard_map/ppermute | solution.py:384
  29.1 15.0 %collective-permute-start.6 = (bf16[320,128]{1,0:T(8,128)(2,1)S(1)}, bf16[320,128]{1,0:T(8,128)(2,1)S(1)}, u32[]{:S(2)}, u32[]{:S(2)}) collective-permute-start(bf16[320,128]{1,0:T(8,128)(2,1)S(1)} %get-tuple-element.47), channel_id=1, source_target_pairs={{0,128},{32,160},{64,192},{96,224},{128,0},{160,32},{192,64},{224,... | collective-permute-start | bytes 245768 | tf_op jit(solution)/shard_map/ppermute | solution.py:384
  35.7 9.0 %copy-start.5 = (s32[128,16]{0,1:T(8,128)S(1)}, s32[128,16]{0,1:T(8,128)}, u32[]{:S(2)}) copy-start(s32[128,16]{0,1:T(8,128)} %param.16) | copy-start | bytes 24580
  44.2 1.9 %collective-permute-start.7 = (bf16[128,1024]{1,0:T(8,128)(2,1)S(1)}, bf16[128,1024]{1,0:T(8,128)(2,1)S(1)}, u32[]{:S(2)}, u32[]{:S(2)}) collective-permute-start(bf16[128,1024]{1,0:T(8,128)(2,1)S(1)} %get-tuple-element.48.own_ref), channel_id=1, source_target_pairs={{0,1},{1,0},{2,3},{3,2},{4,5},{5,4},{6,7},{7,6},{8,9},{9,8},{10,11... | collective-permute-start | bytes 786440 | tf_op jit(solution)/shard_map/ppermute | solution.py:412
  44.7 6.2 %collective-permute-start.8 = (bf16[128,1024]{1,0:T(8,128)(2,1)S(1)}, bf16[128,1024]{1,0:T(8,128)(2,1)S(1)}, u32[]{:S(2)}, u32[]{:S(2)}) collective-permute-start(bf16[128,1024]{1,0:T(8,128)(2,1)S(1)} %get-tuple-element.48.own_ref), channel_id=1, source_target_pairs={{0,31},{1,2},{2,1},{3,4},{4,3},{5,6},{6,5},{7,8},{8,7},{9,10},{10,... | collective-permute-start | bytes 786440 | tf_op jit(solution)/shard_map/ppermute | solution.py:413
  46.1 4.9 %copy-start.2 = (bf16[1024,100]{0,1:T(8,128)(2,1)S(1)}, bf16[1024,100]{0,1:T(8,128)(2,1)}, u32[]{:S(2)}) copy-start(bf16[1024,100]{0,1:T(8,128)(2,1)} %param.23) | copy-start | bytes 614404
  50.9 40.9 %copy-start.3 = (f32[3072]{0:T(1024)S(1)}, f32[3072]{0:T(1024)}, u32[]{:S(2)}) copy-start(f32[3072]{0:T(1024)} %param.25) | copy-start | bytes 36868
  86.8 5.0 %collective-permute-start.9 = (bf16[2048,128]{1,0:T(8,128)(2,1)S(1)}, bf16[2048,128]{1,0:T(8,128)(2,1)S(1)}, u32[]{:S(2)}, u32[]{:S(2)}) collective-permute-start(bf16[2048,128]{1,0:T(8,128)(2,1)S(1)} %bitcast.16), channel_id=1, source_target_pairs={{0,1},{1,0},{2,3},{3,2},{4,5},{5,4},{6,7},{7,6},{8,9},{9,8},{10,11... | collective-permute-start | bytes 1572872 | tf_op jit(solution)/shard_map/ppermute | solution.py:466

commit v4 on v3

--- a/solution.py
+++ b/solution.py
@@ -237,12 +237,13 @@
 
 
 def crps_kernel(member_ref, ids_ref, table_ref, other_ref, seen, area_ref, *rest):
-    *parts, out_ref, table, states, slopes, picked, held = rest
-    members = len(parts)
+    *arrays, table, states, slopes, picked, held = rest
+    members = len(arrays) // 2
+    parts, outs = arrays[:members], arrays[members:]
     names = [(member_ref[0] + members - d) % members for d in range(members)]
     blocks = ids_ref.shape[0]
     per_member = blocks // members
-    rows = out_ref.shape[1]
+    rows = outs[0].shape[0]
     half = table_ref.shape[0]
     table[:half, :] = table_ref[...].astype(F32)
     table[half:, :] = other_ref[...].astype(F32)
@@ -262,7 +263,7 @@
         here = pl.ds(pl.multiple_of(j * LANE, LANE), LANE)
         held[turn * LANE : (turn + 1) * LANE, :] = picked[turn * LANE : (turn + 1) * LANE, :].T
         area = area_ref[pl.ds(j, 1), :]
-        spare = j // per_member * rows + PART * blocks + j % per_member
+        spare = (member_ref[0] + members - j // per_member) % members * rows + PART * blocks + j % per_member
         for low in range(0, PAD, 8):
             count = min(8, PART - low)
             start = turn * LANE + low
@@ -289,7 +290,7 @@
                 r = lax.rsqrt(q)
                 near = q * r if near is None else near + q * r
                 value = area * (miss * r - slope[m] * (1.0 / (members - 1)))
-                slopes[pl.ds(names[m] * rows + low * blocks + j, count, stride=blocks), :] = value[:count]
+                slopes[pl.ds(m * rows + low * blocks + j, count, stride=blocks), :] = value[:count]
             pairs = (2.0 * pairs + 0.1 * members) * (1.0 / (2.0 * members * (members - 1)))
             value = area * (near * (1.0 / members) - pairs)
             slopes[pl.ds(spare + low * per_member, count, stride=per_member), :] = value[:count]
@@ -305,22 +306,33 @@
 
     lax.fori_loop(0, blocks // 2, two, 0)
     for m in range(members):
-        out_ref[m] = slopes[m * rows : (m + 1) * rows, :].astype(BF16)
-
-
-def unpack_kernel(got_ref, crps_ref, grads_ref, wide):
+        outs[m][...] = slopes[m * rows : (m + 1) * rows, :].astype(BF16)
+
+
+def unpack_kernel(member_ref, *rest):
+    *got, crps_ref, grads_ref, wide, scores = rest
     variables, points = crps_ref.shape
-    parts = got_ref.shape[0]
+    parts = len(got)
     per_part = points // LANE
     blocks = parts * per_part
-    for c in range(parts):
-        wide[...] = got_ref[c].astype(F32)
-        held = min(PART, variables - c * PART)
-        grads_ref[c * PART * blocks : (c * PART + held) * blocks, :] = wide[: held * blocks, :]
-        for j in range(per_part):
-            crps_ref[c * PART : c * PART + held, j * LANE : (j + 1) * LANE] = wide[
-                pl.ds(PART * blocks + j, held, stride=per_part), :
-            ]
+    least = variables - (parts - 1) * PART
+    size = parts * PART
+    for d in range(parts):
+        part = (member_ref[0] + d) % parts
+        wide[...] = got[d][...].astype(F32)
+        first = pl.multiple_of(part * (PART * blocks), 8)
+        grads_ref[pl.ds(first, least * blocks), :] = wide[: least * blocks, :]
+
+        @pl.when(part < parts - 1)
+        def _():
+            grads_ref[pl.ds(first + least * blocks, (PART - least) * blocks), :] = wide[least * blocks : PART * blocks, :]
+
+        for v in range(PART):
+            for j in range(per_part):
+                row = PART * blocks + v * per_part + j
+                scores[pl.ds(j * size + part * PART + v, 1), :] = wide[row : row + 1, :]
+    for j in range(per_part):
+        crps_ref[:, j * LANE : (j + 1) * LANE] = scores[j * size : j * size + variables, :]
 
 
 def local(
@@ -467,9 +479,9 @@
     rows = -(-PART * (blocks + blocks // members) // 16) * 16
     slopes = pl.pallas_call(
         crps_kernel,
-        out_shape=shape((members, rows, LANE), BF16),
+        out_shape=[shape((rows, LANE), BF16)] * members,
         in_specs=[SM] * 2 + [VM] * (4 + members),
-        out_specs=VM,
+        out_specs=[VM] * members,
         scratch_shapes=[
             pltpu.VMEM((spaces * nodes, LANE), F32),
             pltpu.VMEM((members * held + (PAD - PART) * blocks, LANE), F32),
@@ -489,17 +501,19 @@
         area.reshape(blocks, LANE),
         *parts,
     )
-    slopes = lax.all_to_all(slopes, "ens", split_axis=0, concat_axis=0, tiled=True)
+    slopes = list(slopes)
+    for d in (4, 3, 5, 2, 6, 1, 7):
+        slopes[d] = lax.ppermute(slopes[d], "ens", [(i, (i - d) % members) for i in range(members)])
     crps, grads = pl.pallas_call(
         unpack_kernel,
         out_shape=(shape((variables, points // members), F32), shape((variables * blocks, LANE), F32)),
-        in_specs=[VM],
+        in_specs=[SM] + [VM] * members,
         out_specs=(VM, VM),
-        scratch_shapes=[pltpu.VMEM((rows, LANE), F32)],
+        scratch_shapes=[pltpu.VMEM((rows, LANE), F32), pltpu.VMEM((PART * blocks, LANE), F32)],
         compiler_params=params(16),
         cost_estimate=cost(1e6, 2e6),
         name="unpack",
-    )(slopes)
+    )(member.astype(jnp.int32).reshape(1), *slopes)
     return crps, grads.reshape(1, variables, points)
 
 

time: 124 us -> 124 us (level)
  blocking collectives: 54.2 us -> 29.6 us
  waiting for transfers between devices: 4.93 us -> 19.4 us
  starting transfers between devices: 31.5 us -> 41.1 us
    all_to_all x1 -> x0, blocking collectives: 24.6 us -> none  [local(): lax.all_to_all(slopes, 'ens', split_axis=0, concat_axis=0, tiled=True)]
    ppermute x0 -> x7, waiting for transfers between devices: none -> 14.5 us  [local(): lax.ppermute(slopes[d], 'ens', [(i, (i - d) % members) for i in range(mem...]
    ppermute x0 -> x7, starting transfers between devices: none -> 9.58 us  [local(): lax.ppermute(slopes[d], 'ens', [(i, (i - d) % members) for i in range(mem...]
  transfers between devices with their start and end apart: 11 -> 18, of which waited for: 3 -> 6; matrix products, arithmetic and copies ran while one was open for 0% -> 0% of each run, Pallas kernels for 10% -> 10%
where the time goes in v4:
time: 124 us
  starting transfers between devices  41.1 us (33%)
  Pallas kernels  32.2 us (26%)
  blocking collectives  29.6 us (24%)
  waiting for transfers between devices  19.4 us (16%)
    ppermute x7, starting transfers between devices, local(): lax.ppermute(parts[d], 'ens', [(i, (i + d) % members) for i in range(memb...  17.7 us
    all_to_all x1, blocking collectives, local(): lax.all_to_all(decoded, 'ens', split_axis=0, concat_axis=0, tiled=True)  14.9 us
    all_to_all x1, blocking collectives, local(): lax.all_to_all(jnp.broadcast_to(decoded[None], (spaces // 2, nodes, membe...  14.8 us
    ppermute x7, waiting for transfers between devices, local(): lax.ppermute(slopes[d], 'ens', [(i, (i - d) % members) for i in range(mem...  14.5 us
    ppermute x7, starting transfers between devices, local(): lax.ppermute(slopes[d], 'ens', [(i, (i - d) % members) for i in range(mem...  9.58 us
    all_to_all x1, starting transfers between devices, local(): lax.all_to_all(slots.reshape(spaces, SENT, LANE), 'space', split_axis=0,...  8.6 us
    pallas_call x1, Pallas kernels, local(): pl.pallas_call(encode_kernel, out_shape=(shape((nodes, width), BF16), sha...  8.42 us
    pallas_call x1, Pallas kernels, local(): pl.pallas_call(pack_kernel, out_shape=(shape((spaces * SENT, LANE), BF16)...  6.5 us
  transfers between devices with their start and end apart: 18, of which 6 were waited for; matrix products, arithmetic and copies ran while one was open for 0% of the time, Pallas kernels for 10%

profile of v4, /device:TPU:1, one launch (start us, length us, event | category | flops | bytes accessed | tf_op | source)
XLA Modules:
  0.0 123.7 jit_solution(11870051475237440100)
XLA Ops:
  0.7 0.1 pad_add_fusion.core_ref
  0.7 6.5 %pack.1 = (bf16[5120,128]{1,0:T(8,128)(2,1)}, s32[24,128]{1,0:T(8,128)S(1)}, bf16[320,128]{1,0:T(8,128)(2,1)S(1)}, bf16[320,128]{1,0:T(8,128)(2,1)S(1)}, bf16[32...) custom-call(s32[2]{0:T(128)S(1)} %pad_add_fusion.core_ref, ...), custom_call_target="tpu_custom_call" | custom-call | flops 150000000 | bytes 8000000 | tf_op jit(solution)/shard_map/pack/pallas_call | solution.py:364
  7.3 8.6 %all-to-all-start = ((bf16[32,160,128]{2,1,0:T(8,128)(2,1)}), bf16[32,160,128]{2,1,0:T(8,128)(2,1)S(1)}, u32[]{:S(2)}, u32[]{:S(2)}) async-start(bf16[32,160,128]{2,1,0:T(8,128)(2,1)} %bitcast.5), calls=%async_computation | async-start | bytes 2621440 | tf_op jit(solution)/shard_map/all_to_all | solution.py:394
  15.9 4.4 %collective-permute-start = (bf16[320,128]{1,0:T(8,128)(2,1)S(1)}, bf16[320,128]{1,0:T(8,128)(2,1)S(1)}, u32[]{:S(2)}, u32[]{:S(2)}) collective-permute-start(bf16[320,128]{1,0:T(8,128)(2,1)S(1)} %get-tuple-element.46), channel_id=1, source_target_pairs={{0,96},{32,128},{64,160},{96,192},{128,224},{160,0},{192,32},{224,... | collective-permute-start | bytes 245768 | tf_op jit(solution)/shard_map/ppermute | solution.py:396
  20.3 2.2 %collective-permute-start.1 = (bf16[320,128]{1,0:T(8,128)(2,1)S(1)}, bf16[320,128]{1,0:T(8,128)(2,1)S(1)}, u32[]{:S(2)}, u32[]{:S(2)}) collective-permute-start(bf16[320,128]{1,0:T(8,128)(2,1)S(1)} %get-tuple-element.47), channel_id=1, source_target_pairs={{0,160},{32,192},{64,224},{96,0},{128,32},{160,64},{192,96},{224,1... | collective-permute-start | bytes 245768 | tf_op jit(solution)/shard_map/ppermute | solution.py:396
  22.5 1.2 collective-permute-start.2
  23.7 2.7 %collective-permute-start.3 = (bf16[320,128]{1,0:T(8,128)(2,1)S(1)}, bf16[320,128]{1,0:T(8,128)(2,1)S(1)}, u32[]{:S(2)}, u32[]{:S(2)}) collective-permute-start(bf16[320,128]{1,0:T(8,128)(2,1)S(1)} %get-tuple-element.52), channel_id=1, source_target_pairs={{0,192},{32,224},{64,0},{96,32},{128,64},{160,96},{192,128},{224,1... | collective-permute-start | bytes 245768 | tf_op jit(solution)/shard_map/ppermute | solution.py:396
  26.4 0.4 collective-permute-start.4
  26.8 0.0 collective-permute-done.rest_3_
  26.8 2.3 %collective-permute-start.5 = (bf16[320,128]{1,0:T(8,128)(2,1)S(1)}, bf16[320,128]{1,0:T(8,128)(2,1)S(1)}, u32[]{:S(2)}, u32[]{:S(2)}) collective-permute-start(bf16[320,128]{1,0:T(8,128)(2,1)S(1)} %get-tuple-element.54), channel_id=1, source_target_pairs={{0,224},{32,0},{64,32},{96,64},{128,96},{160,128},{192,160},{224,1... | collective-permute-start | bytes 245768 | tf_op jit(solution)/shard_map/ppermute | solution.py:396
  29.1 0.0 collective-permute-done.1.rest_5_
  29.1 4.5 %collective-permute-start.6 = (bf16[320,128]{1,0:T(8,128)(2,1)S(1)}, bf16[320,128]{1,0:T(8,128)(2,1)S(1)}, u32[]{:S(2)}, u32[]{:S(2)}) collective-permute-start(bf16[320,128]{1,0:T(8,128)(2,1)S(1)} %get-tuple-element.55), channel_id=1, source_target_pairs={{0,128},{32,160},{64,192},{96,224},{128,0},{160,32},{192,64},{224,... | collective-permute-start | bytes 245768 | tf_op jit(solution)/shard_map/ppermute | solution.py:396
  33.6 2.1 %all-to-all-done = bf16[32,160,128]{2,1,0:T(8,128)(2,1)S(1)} async-done(((bf16[32,160,128]{2,1,0:T(8,128)(2,1)}), bf16[32,160,128]{2,1,0:T(8,128)(2,1)S(1)}, u32[]{:S(2)}, u32[]{:S(2)}) %all-to-all-start) | async-done | bytes 1310752 | tf_op jit(solution)/shard_map/all_to_all | solution.py:394
  35.7 0.0 copy-start.5
  35.7 8.4 %encode.1 = (bf16[128,1024]{1,0:T(8,128)(2,1)S(1)}, bf16[128,1024]{1,0:T(8,128)(2,1)S(1)}) custom-call(bf16[5120,128]{1,0:T(8,128)(2,1)S(1)} %bitcast.15, bf16[100,1024]{1,0:T(8,128)(2,1)S(1)} %copy-done.1, bf16[128,1024]{1,0:T(8,128)(2,1)S(1)} %copy-done, f32[1,1024]{1,0:T(1,128)S(1)} %bitcast.20, bf16[1024,1024]{1,0:T(8,128)(2,1)} %sender_ref.1), custom_call_target="tpu_custom_call" | custom-call | flops 4000000000 | bytes 8000000 | tf_op jit(solution)/shard_map/encode/pallas_call | solution.py:401
  44.1 0.0 collective-permute-done.2.rest_2_
  44.1 0.0 collective-permute-done.3.rest_6_
  44.1 0.0 collective-permute-done.4.rest_1_
  44.1 0.0 collective-permute-done.5.rest_7_
  44.2 0.5 collective-permute-start.7
  44.6 0.1 copy.21
  44.7 1.2 %collective-permute-start.8 = (bf16[128,1024]{1,0:T(8,128)(2,1)S(1)}, bf16[128,1024]{1,0:T(8,128)(2,1)S(1)}, u32[]{:S(2)}, u32[]{:S(2)}) collective-permute-start(bf16[128,1024]{1,0:T(8,128)(2,1)S(1)} %get-tuple-element.56.own_ref), channel_id=1, source_target_pairs={{0,31},{1,2},{2,1},{3,4},{4,3},{5,6},{6,5},{7,8},{8,7},{9,10},{10,... | collective-permute-start | bytes 786440 | tf_op jit(solution)/shard_map/ppermute | solution.py:425
  46.0 0.1 fusion.near_ref
  46.1 0.0 collective-permute-done.7.sibling_ref
  46.1 0.0 copy-start.2
  46.1 3.5 %near.1 = (f32[2048,1024]{1,0:T(8,128)S(1)}, f32[16,3072]{1,0:T(8,128)S(1)}, bf16[1024,1024]{1,0:T(8,128)(2,1)S(1)}) custom-call(s32[1]{0:T(128)} %bitcast.member_ref, s32[128,16]{1,0:T(8,128)S(1)} %fusion.near_ref, bf16[128,1024]{1,0:T(8,128)(2,1)S(1)} %get-tuple-element.49.normed_ref, bf16[128,1024]{1,0:T(8,128)(2,1)S(1)} %collective-permute-done.7.sibling_ref, ...), custom_call_target="tpu_custom_call" | custom-call | flops 2000000000 | bytes 4000000 | tf_op jit(solution)/shard_map/near/pallas_call | solution.py:429
  49.6 1.3 %collective-permute-done.8.other_ref = bf16[128,1024]{1,0:T(8,128)(2,1)S(1)} collective-permute-done((bf16[128,1024]{1,0:T(8,128)(2,1)S(1)}, bf16[128,1024]{1,0:T(8,128)(2,1)S(1)}, u32[]{:S(2)}, u32[]{:S(2)}) %collective-permute-start.8) | collective-permute-done | bytes 262176 | tf_op jit(solution)/shard_map/ppermute | solution.py:425
  50.9 6.0 %process.1 = bf16[8,16,128]{2,1,0:T(8,128)(2,1)S(1)} custom-call(s32[128,16]{1,0:T(8,128)S(1)} %fusion.near_ref, f32[2048,1024]{1,0:T(8,128)S(1)} %get-tuple-element.57.half_ref, bf16[128,1024]{1,0:T(8,128)(2,1)S(1)} %get-tuple-element.49.normed_ref, bf16[128,1024]{1,0:T(8,128)(2,1)S(1)} %collective-permute-done.8.other_ref, ...), custom_call_target="tpu_custom_call" | custom-call | flops 6000000000 | bytes 4000000 | tf_op jit(solution)/shard_map/process/pallas_call | solution.py:453
  56.9 14.9 %all_to_all.15 = bf16[8,16,128]{2,1,0:T(8,128)(2,1)S(1)} all-to-all(bf16[8,16,128]{2,1,0:T(8,128)(2,1)S(1)} %process.1), channel_id=1, replica_groups=mesh['ens'=8,'space'=32] {'ens'}, dimensions={0} | all-to-all | bytes 65536 | tf_op jit(solution)/shard_map/all_to_all | solution.py:468
  71.8 0.1 copy.25
  71.9 0.1 broadcast_in_dim.15
  72.0 14.8 %all_to_all.16 = bf16[16,128,128]{2,1,0:T(8,128)(2,1)S(1)} all-to-all(bf16[16,128,128]{2,1,0:T(8,128)(2,1)S(1)} %broadcast_in_dim.15), channel_id=1, replica_groups={{0,2,4,6,8,10,12,14,16,18,20,22,24,26,28,30},{1,3,5,7,9,11,13,15,17,19,..., dimensions={0} | all-to-all | bytes 1048576 | tf_op jit(solution)/shard_map/all_to_all | solution.py:470
  86.8 3.5 %collective-permute-start.9 = (bf16[2048,128]{1,0:T(8,128)(2,1)S(1)}, bf16[2048,128]{1,0:T(8,128)(2,1)S(1)}, u32[]{:S(2)}, u32[]{:S(2)}) collective-permute-start(bf16[2048,128]{1,0:T(8,128)(2,1)S(1)} %bitcast.16), channel_id=1, source_target_pairs={{0,1},{1,0},{2,3},{3,2},{4,5},{5,4},{6,7},{7,6},{8,9},{9,8},{10,11... | collective-permute-start | bytes 1572872 | tf_op jit(solution)/shard_map/ppermute | solution.py:478
  90.3 1.5 %collective-permute-done.9.other_ref = bf16[2048,128]{1,0:T(8,128)(2,1)S(1)} collective-permute-done((bf16[2048,128]{1,0:T(8,128)(2,1)S(1)}, bf16[2048,128]{1,0:T(8,128)(2,1)S(1)}, u32[]{:S(2)}, u32[]{:S(2)}) %collective-permute-start.9) | collective-permute-done | bytes 524320 | tf_op jit(solution)/shard_map/ppermute | solution.py:478
  91.8 6.5 %crps.1 = (bf16[352,128]{1,0:T(8,128)(2,1)S(1)}, bf16[352,128]{1,0:T(8,128)(2,1)S(1)}, bf16[352,128]{1,0:T(8,128)(2,1)S(1)}, bf16[352,128]{1,0:T(8,128)(2,1)S(1)...) custom-call(s32[1]{0:T(128)} %bitcast.member_ref, ...), custom_call_target="tpu_custom_call" | custom-call | flops 5000000000 | bytes 6000000 | tf_op jit(solution)/shard_map/crps/pallas_call | solution.py:480
  98.3 0.2 collective-permute-start.10
  98.5 0.4 collective-permute-start.11
  98.8 3.2 %collective-permute-start.12 = (bf16[352,128]{1,0:T(8,128)(2,1)S(1)}, bf16[352,128]{1,0:T(8,128)(2,1)S(1)}, u32[]{:S(2)}, u32[]{:S(2)}) collective-permute-start(bf16[352,128]{1,0:T(8,128)(2,1)S(1)} %get-tuple-element.79), channel_id=1, source_target_pairs={{0,160},{32,192},{64,224},{96,0},{128,32},{160,64},{192,96},{224,1... | collective-permute-start | bytes 270344 | tf_op jit(solution)/shard_map/ppermute | solution.py:506
  102.1 2.2 %collective-permute-start.13 = (bf16[352,128]{1,0:T(8,128)(2,1)S(1)}, bf16[352,128]{1,0:T(8,128)(2,1)S(1)}, u32[]{:S(2)}, u32[]{:S(2)}) collective-permute-start(bf16[352,128]{1,0:T(8,128)(2,1)S(1)} %get-tuple-element.80), channel_id=1, source_target_pairs={{0,128},{32,160},{64,192},{96,224},{128,0},{160,32},{192,64},{224,... | collective-permute-start | bytes 270344 | tf_op jit(solution)/shard_map/ppermute | solution.py:506
  104.3 2.1 %collective-permute-start.14 = (bf16[352,128]{1,0:T(8,128)(2,1)S(1)}, bf16[352,128]{1,0:T(8,128)(2,1)S(1)}, u32[]{:S(2)}, u32[]{:S(2)}) collective-permute-start(bf16[352,128]{1,0:T(8,128)(2,1)S(1)} %get-tuple-element.81), channel_id=1, source_target_pairs={{0,96},{32,128},{64,160},{96,192},{128,224},{160,0},{192,32},{224,... | collective-permute-start | bytes 270344 | tf_op jit(solution)/shard_map/ppermute | solution.py:506
  106.4 0.0 collective-permute-done.10.rest_1_
  106.4 1.5 %collective-permute-start.15 = (bf16[352,128]{1,0:T(8,128)(2,1)S(1)}, bf16[352,128]{1,0:T(8,128)(2,1)S(1)}, u32[]{:S(2)}, u32[]{:S(2)}) collective-permute-start(bf16[352,128]{1,0:T(8,128)(2,1)S(1)} %get-tuple-element.82), channel_id=1, source_target_pairs={{0,64},{32,96},{64,128},{96,160},{128,192},{160,224},{192,0},{224,... | collective-permute-start | bytes 270344 | tf_op jit(solution)/shard_map/ppermute | solution.py:506
  107.9 0.0 collective-permute-done.11.rest_2_
  107.9 1.5 %collective-permute-done.13.rest_4_ = bf16[352,128]{1,0:T(8,128)(2,1)S(1)} collective-permute-done((bf16[352,128]{1,0:T(8,128)(2,1)S(1)}, bf16[352,128]{1,0:T(8,128)(2,1)S(1)}, u32[]{:S(2)}, u32[]{:S(2)}) %collective-permute-start.13) | collective-permute-done | bytes 90144 | tf_op jit(solution)/shard_map/ppermute | solution.py:506
  109.4 9.3 %collective-permute-done.14.rest_5_ = bf16[352,128]{1,0:T(8,128)(2,1)S(1)} collective-permute-done((bf16[352,128]{1,0:T(8,128)(2,1)S(1)}, bf16[352,128]{1,0:T(8,128)(2,1)S(1)}, u32[]{:S(2)}, u32[]{:S(2)}) %collective-permute-start.14) | collective-permute-done | bytes 90144 | tf_op jit(solution)/shard_map/ppermute | solution.py:506
  118.7 0.0 collective-permute-done.15.rest_6_
  118.7 3.7 %collective-permute-done.16.rest_7_ = bf16[352,128]{1,0:T(8,128)(2,1)S(1)} collective-permute-done((bf16[352,128]{1,0:T(8,128)(2,1)S(1)}, bf16[352,128]{1,0:T(8,128)(2,1)S(1)}, u32[]{:S(2)}, u32[]{:S(2)}) %collective-permute-start.16) | collective-permute-done | bytes 90144 | tf_op jit(solution)/shard_map/ppermute | solution.py:506
  122.4 1.3 %unpack.1 = (f32[100,384]{1,0:T(8,128)}, f32[2400,128]{1,0:T(8,128)}) custom-call(s32[1]{0:T(128)} %bitcast.member_ref, bf16[352,128]{1,0:T(8,128)(2,1)S(1)} %get-tuple-element.76.rest_0_, bf16[352,128]{1,0:T(8,128)(2,1)S(1)} %collective-permute-done.10.rest_1_, bf16[352,128]{1,0:T(8,128)(2,1)S(1)} %collective-permute-done.11.rest_2_, ...), custom_call_target="tpu_custom_call" | custom-call | flops 1000000 | bytes 2000000 | tf_op jit(solution)/shard_map/unpack/pallas_call | solution.py:507
  (13 shorter events, 0.0 us)
Async XLA Ops:
  0.6 35.0 %copy-start.4 = (f32[1024]{0:T(1024)S(1)}, f32[1024]{0:T(1024)}, u32[]{:S(2)}) copy-start(f32[1024]{0:T(1024)} %param.18) | copy-start | bytes 12292
  0.6 35.0 %copy-start = (bf16[128,1024]{1,0:T(8,128)(2,1)S(1)}, bf16[128,1024]{1,0:T(8,128)(2,1)}, u32[]{:S(2)}) copy-start(bf16[128,1024]{1,0:T(8,128)(2,1)} %latent_ref.1) | copy-start | bytes 786436
  0.7 35.0 %copy-start.1 = (bf16[100,1024]{1,0:T(8,128)(2,1)S(1)}, bf16[100,1024]{1,0:T(8,128)(2,1)}, u32[]{:S(2)}) copy-start(bf16[100,1024]{1,0:T(8,128)(2,1)} %embed_ref.1) | copy-start | bytes 614404
  7.3 28.4 %all-to-all-start = ((bf16[32,160,128]{2,1,0:T(8,128)(2,1)}), bf16[32,160,128]{2,1,0:T(8,128)(2,1)S(1)}, u32[]{:S(2)}, u32[]{:S(2)}) async-start(bf16[32,160,128]{2,1,0:T(8,128)(2,1)} %bitcast.5), calls=%async_computation | async-start | bytes 2621440 | tf_op jit(solution)/shard_map/all_to_all | solution.py:394
  15.9 11.0 %collective-permute-start = (bf16[320,128]{1,0:T(8,128)(2,1)S(1)}, bf16[320,128]{1,0:T(8,128)(2,1)S(1)}, u32[]{:S(2)}, u32[]{:S(2)}) collective-permute-start(bf16[320,128]{1,0:T(8,128)(2,1)S(1)} %get-tuple-element.46), channel_id=1, source_target_pairs={{0,96},{32,128},{64,160},{96,192},{128,224},{160,0},{192,32},{224,... | collective-permute-start | bytes 245768 | tf_op jit(solution)/shard_map/ppermute | solution.py:396
  20.3 8.8 %collective-permute-start.1 = (bf16[320,128]{1,0:T(8,128)(2,1)S(1)}, bf16[320,128]{1,0:T(8,128)(2,1)S(1)}, u32[]{:S(2)}, u32[]{:S(2)}) collective-permute-start(bf16[320,128]{1,0:T(8,128)(2,1)S(1)} %get-tuple-element.47), channel_id=1, source_target_pairs={{0,160},{32,192},{64,224},{96,0},{128,32},{160,64},{192,96},{224,1... | collective-permute-start | bytes 245768 | tf_op jit(solution)/shard_map/ppermute | solution.py:396
  22.5 21.6 %collective-permute-start.2 = (bf16[320,128]{1,0:T(8,128)(2,1)S(1)}, bf16[320,128]{1,0:T(8,128)(2,1)S(1)}, u32[]{:S(2)}, u32[]{:S(2)}) collective-permute-start(bf16[320,128]{1,0:T(8,128)(2,1)S(1)} %get-tuple-element.51), channel_id=1, source_target_pairs={{0,64},{32,96},{64,128},{96,160},{128,192},{160,224},{192,0},{224,... | collective-permute-start | bytes 245768 | tf_op jit(solution)/shard_map/ppermute | solution.py:396
  23.7 20.4 %collective-permute-start.3 = (bf16[320,128]{1,0:T(8,128)(2,1)S(1)}, bf16[320,128]{1,0:T(8,128)(2,1)S(1)}, u32[]{:S(2)}, u32[]{:S(2)}) collective-permute-start(bf16[320,128]{1,0:T(8,128)(2,1)S(1)} %get-tuple-element.52), channel_id=1, source_target_pairs={{0,192},{32,224},{64,0},{96,32},{128,64},{160,96},{192,128},{224,1... | collective-permute-start | bytes 245768 | tf_op jit(solution)/shard_map/ppermute | solution.py:396
  26.4 17.7 %collective-permute-start.4 = (bf16[320,128]{1,0:T(8,128)(2,1)S(1)}, bf16[320,128]{1,0:T(8,128)(2,1)S(1)}, u32[]{:S(2)}, u32[]{:S(2)}) collective-permute-start(bf16[320,128]{1,0:T(8,128)(2,1)S(1)} %get-tuple-element.53), channel_id=1, source_target_pairs={{0,32},{32,64},{64,96},{96,128},{128,160},{160,192},{192,224},{224... | collective-permute-start | bytes 245768 | tf_op jit(solution)/shard_map/ppermute | solution.py:396
  26.8 17.3 %collective-permute-start.5 = (bf16[320,128]{1,0:T(8,128)(2,1)S(1)}, bf16[320,128]{1,0:T(8,128)(2,1)S(1)}, u32[]{:S(2)}, u32[]{:S(2)}) collective-permute-start(bf16[320,128]{1,0:T(8,128)(2,1)S(1)} %get-tuple-element.54), channel_id=1, source_target_pairs={{0,224},{32,0},{64,32},{96,64},{128,96},{160,128},{192,160},{224,1... | collective-permute-start | bytes 245768 | tf_op jit(solution)/shard_map/ppermute | solution.py:396
  29.1 15.0 %collective-permute-start.6 = (bf16[320,128]{1,0:T(8,128)(2,1)S(1)}, bf16[320,128]{1,0:T(8,128)(2,1)S(1)}, u32[]{:S(2)}, u32[]{:S(2)}) collective-permute-start(bf16[320,128]{1,0:T(8,128)(2,1)S(1)} %get-tuple-element.55), channel_id=1, source_target_pairs={{0,128},{32,160},{64,192},{96,224},{128,0},{160,32},{192,64},{224,... | collective-permute-start | bytes 245768 | tf_op jit(solution)/shard_map/ppermute | solution.py:396
  35.7 9.0 %copy-start.5 = (s32[128,16]{0,1:T(8,128)S(1)}, s32[128,16]{0,1:T(8,128)}, u32[]{:S(2)}) copy-start(s32[128,16]{0,1:T(8,128)} %param.16) | copy-start | bytes 24580
  44.2 1.9 %collective-permute-start.7 = (bf16[128,1024]{1,0:T(8,128)(2,1)S(1)}, bf16[128,1024]{1,0:T(8,128)(2,1)S(1)}, u32[]{:S(2)}, u32[]{:S(2)}) collective-permute-start(bf16[128,1024]{1,0:T(8,128)(2,1)S(1)} %get-tuple-element.56.own_ref), channel_id=1, source_target_pairs={{0,1},{1,0},{2,3},{3,2},{4,5},{5,4},{6,7},{7,6},{8,9},{9,8},{10,11... | collective-permute-start | bytes 786440 | tf_op jit(solution)/shard_map/ppermute | solution.py:424
  44.7 6.2 %collective-permute-start.8 = (bf16[128,1024]{1,0:T(8,128)(2,1)S(1)}, bf16[128,1024]{1,0:T(8,128)(2,1)S(1)}, u32[]{:S(2)}, u32[]{:S(2)}) collective-permute-start(bf16[128,1024]{1,0:T(8,128)(2,1)S(1)} %get-tuple-element.56.own_ref), channel_id=1, source_target_pairs={{0,31},{1,2},{2,1},{3,4},{4,3},{5,6},{6,5},{7,8},{8,7},{9,10},{10,... | collective-permute-start | bytes 786440 | tf_op jit(solution)/shard_map/ppermute | solution.py:425
  46.1 4.8 %copy-start.2 = (bf16[1024,100]{0,1:T(8,128)(2,1)S(1)}, bf16[1024,100]{0,1:T(8,128)(2,1)}, u32[]{:S(2)}) copy-start(bf16[1024,100]{0,1:T(8,128)(2,1)} %param.23) | copy-start | bytes 614404
  50.9 40.9 %copy-start.3 = (f32[3072]{0:T(1024)S(1)}, f32[3072]{0:T(1024)}, u32[]{:S(2)}) copy-start(f32[3072]{0:T(1024)} %param.25) | copy-start | bytes 36868
  86.8 5.0 %collective-permute-start.9 = (bf16[2048,128]{1,0:T(8,128)(2,1)S(1)}, bf16[2048,128]{1,0:T(8,128)(2,1)S(1)}, u32[]{:S(2)}, u32[]{:S(2)}) collective-permute-start(bf16[2048,128]{1,0:T(8,128)(2,1)S(1)} %bitcast.16), channel_id=1, source_target_pairs={{0,1},{1,0},{2,3},{3,2},{4,5},{5,4},{6,7},{7,6},{8,9},{9,8},{10,11... | collective-permute-start | bytes 1572872 | tf_op jit(solution)/shard_map/ppermute | solution.py:478
  98.3 8.1 %collective-permute-start.10 = (bf16[352,128]{1,0:T(8,128)(2,1)S(1)}, bf16[352,128]{1,0:T(8,128)(2,1)S(1)}, u32[]{:S(2)}, u32[]{:S(2)}) collective-permute-start(bf16[352,128]{1,0:T(8,128)(2,1)S(1)} %get-tuple-element.77), channel_id=1, source_target_pairs={{0,224},{32,0},{64,32},{96,64},{128,96},{160,128},{192,160},{224,1... | collective-permute-start | bytes 270344 | tf_op jit(solution)/shard_map/ppermute | solution.py:506
  98.5 9.4 %collective-permute-start.11 = (bf16[352,128]{1,0:T(8,128)(2,1)S(1)}, bf16[352,128]{1,0:T(8,128)(2,1)S(1)}, u32[]{:S(2)}, u32[]{:S(2)}) collective-permute-start(bf16[352,128]{1,0:T(8,128)(2,1)S(1)} %get-tuple-element.78), channel_id=1, source_target_pairs={{0,192},{32,224},{64,0},{96,32},{128,64},{160,96},{192,128},{224,1... | collective-permute-start | bytes 270344 | tf_op jit(solution)/shard_map/ppermute | solution.py:506
  98.8 9.0 %collective-permute-start.12 = (bf16[352,128]{1,0:T(8,128)(2,1)S(1)}, bf16[352,128]{1,0:T(8,128)(2,1)S(1)}, u32[]{:S(2)}, u32[]{:S(2)}) collective-permute-start(bf16[352,128]{1,0:T(8,128)(2,1)S(1)} %get-tuple-element.79), channel_id=1, source_target_pairs={{0,160},{32,192},{64,224},{96,0},{128,32},{160,64},{192,96},{224,1... | collective-permute-start | bytes 270344 | tf_op jit(solution)/shard_map/ppermute | solution.py:506
  102.1 7.3 %collective-permute-start.13 = (bf16[352,128]{1,0:T(8,128)(2,1)S(1)}, bf16[352,128]{1,0:T(8,128)(2,1)S(1)}, u32[]{:S(2)}, u32[]{:S(2)}) collective-permute-start(bf16[352,128]{1,0:T(8,128)(2,1)S(1)} %get-tuple-element.80), channel_id=1, source_target_pairs={{0,128},{32,160},{64,192},{96,224},{128,0},{160,32},{192,64},{224,... | collective-permute-start | bytes 270344 | tf_op jit(solution)/shard_map/ppermute | solution.py:506
  104.3 14.4 %collective-permute-start.14 = (bf16[352,128]{1,0:T(8,128)(2,1)S(1)}, bf16[352,128]{1,0:T(8,128)(2,1)S(1)}, u32[]{:S(2)}, u32[]{:S(2)}) collective-permute-start(bf16[352,128]{1,0:T(8,128)(2,1)S(1)} %get-tuple-element.81), channel_id=1, source_target_pairs={{0,96},{32,128},{64,160},{96,192},{128,224},{160,0},{192,32},{224,... | collective-permute-start | bytes 270344 | tf_op jit(solution)/shard_map/ppermute | solution.py:506
  106.4 12.3 %collective-permute-start.15 = (bf16[352,128]{1,0:T(8,128)(2,1)S(1)}, bf16[352,128]{1,0:T(8,128)(2,1)S(1)}, u32[]{:S(2)}, u32[]{:S(2)}) collective-permute-start(bf16[352,128]{1,0:T(8,128)(2,1)S(1)} %get-tuple-element.82), channel_id=1, source_target_pairs={{0,64},{32,96},{64,128},{96,160},{128,192},{160,224},{192,0},{224,... | collective-permute-start | bytes 270344 | tf_op jit(solution)/shard_map/ppermute | solution.py:506
  107.9 14.5 %collective-permute-start.16 = (bf16[352,128]{1,0:T(8,128)(2,1)S(1)}, bf16[352,128]{1,0:T(8,128)(2,1)S(1)}, u32[]{:S(2)}, u32[]{:S(2)}) collective-permute-start(bf16[352,128]{1,0:T(8,128)(2,1)S(1)} %get-tuple-element.83), channel_id=1, source_target_pairs={{0,32},{32,64},{64,96},{96,128},{128,160},{160,192},{192,224},{224... | collective-permute-start | bytes 270344 | tf_op jit(solution)/shard_map/ppermute | solution.py:506
